TPU v7x, 32 devices: a whole 2x2x4 slice. The times are simulated.
32 devices in a mesh: wide: 8 (over z, y), narrow: 4 (over x, core).
Axes of the slice: x: 2, y: 2, z: 4, core: 2. Of those that a mesh axis runs over, the one named last changes fastest.
Arguments:
- target_slot: int32 [1024], replicated, may hold values from 0 to 1023, as said below
- fields: bfloat16 [1024, 8, 4096], P(('wide', 'narrow')), as said below
Outputs:
- migrated: bfloat16 [1024, 8, 4096], P(('wide', 'narrow'))
- pressure: float32 [64, 512, 128], P('narrow', 'wide')
Inputs may be any that keep to these rules, and one draw needn't show every extreme that they name: `target_slot`: A permutation of the patches. Owner w * 4 + n holds patches w * 4 + n times 32 onward, old and new. From one owner to any owner go at most 2 patches, and exactly 2 for some pairs in every draw; every owner receives exactly 32 patches. `fields`: fields 0, 1, 2 are velocity components along the three dimensions, field 3 is the density, between 0.6 and 8.1; the others are carried quantities.
All inputs are finite; a program needn't handle non-finite values.
Results may differ from a plain program's by a relative error of at most 0.0014.
Values may be sent and summed in bfloat16 or wider, within the bound.
A program may use at most 128 MiB of HBM per device.

v0:
```python
import jax
import jax.numpy as jnp
from jax import lax
from jax.sharding import PartitionSpec as P

PATCH = 16
BXP = 1
BYP = 4
BZP = 8
LEVELS = 3
BOTTOM = 16


DAMPING = 0.8


def padded_2(x, sides, width):
    for axis, dim in sides:
        size, length = (lax.axis_size(axis), x.shape[dim])
        up = [(i, (i + 1) % size) for i in range(size - 1)]
        down = [(j, i) for i, j in up]
        last = lax.slice_in_dim(x, length - width, length, axis=dim)
        initial = lax.slice_in_dim(x, 0, width, axis=dim)
        before = lax.ppermute(last, axis, up)
        after = lax.ppermute(initial, axis, down)
        x = jnp.concatenate([before, x, after], axis=dim)
    return x


def neighbours(values, direction):
    length = values.shape[direction]
    zero_plane = jnp.zeros_like(lax.slice_in_dim(values, 0, 1, axis=direction))
    lower_side = jnp.concatenate(
        [zero_plane, lax.slice_in_dim(values, 0, length - 1, axis=direction)], direction
    )
    upper_side = jnp.concatenate(
        [lax.slice_in_dim(values, 1, length, axis=direction), zero_plane], direction
    )
    return (lower_side, upper_side)


def face_along(density, direction):
    zero_plane = jnp.zeros_like(lax.slice_in_dim(density, 0, 1, axis=direction))
    padded = jnp.concatenate([zero_plane, density, zero_plane], direction)
    length = padded.shape[direction]
    return 2.0 / (
        lax.slice_in_dim(padded, 0, length - 1, axis=direction)
        + lax.slice_in_dim(padded, 1, length, axis=direction)
    )


def split_faces(face, direction):
    length = face.shape[direction]
    return (
        lax.slice_in_dim(face, 0, length - 1, axis=direction),
        lax.slice_in_dim(face, 1, length, axis=direction),
    )


def combine_terms(values, neighbour_pairs, face_set, level_scale):
    running = None
    for direction in range(3):
        lower_side, upper_side = neighbour_pairs[direction]
        low_face, high_face = split_faces(face_set[direction], direction)
        face_term = high_face * (values - upper_side) + low_face * (values - lower_side)
        running = face_term if running is None else running + face_term
    return level_scale * running


def apply_padded(values, face_set, level_scale):
    neighbour_pairs = tuple((neighbours(values, direction) for direction in range(3)))
    return combine_terms(values, neighbour_pairs, face_set, level_scale)


def rimmed(values):
    return padded_2(values, (("wide", 1), ("narrow", 0)), 1)


def apply_rimmed(values, face_set, level_scale):
    padded = rimmed(values)
    neighbour_pairs = (
        (padded[:-2, 1:-1], padded[2:, 1:-1]),
        (padded[1:-1, :-2], padded[1:-1, 2:]),
        neighbours(values, 2),
    )
    return combine_terms(values, neighbour_pairs, face_set, level_scale)


def diagonal_of(face_set, level_scale):
    running = None
    for direction in range(3):
        low_face, high_face = split_faces(face_set[direction], direction)
        face_term = low_face + high_face
        running = face_term if running is None else running + face_term
    return level_scale * running


def coarsen_faces(face_set):
    face_x, face_y, face_z = face_set
    picked = face_x[::2]
    coarse_x = picked.reshape(
        picked.shape[0], picked.shape[1] // 2, 2, picked.shape[2] // 2, 2
    ).mean(axis=(2, 4))
    picked = face_y[:, ::2]
    coarse_y = picked.reshape(
        picked.shape[0] // 2, 2, picked.shape[1], picked.shape[2] // 2, 2
    ).mean(axis=(1, 4))
    picked = face_z[:, :, ::2]
    coarse_z = picked.reshape(
        picked.shape[0] // 2, 2, picked.shape[1] // 2, 2, picked.shape[2]
    ).mean(axis=(1, 3))
    return (coarse_x, coarse_y, coarse_z)


def restrict_mean(values):
    shape = values.shape
    return values.reshape(shape[0] // 2, 2, shape[1] // 2, 2, shape[2] // 2, 2).mean(axis=(1, 3, 5))


def prolong(values):
    return jnp.repeat(jnp.repeat(jnp.repeat(values, 2, axis=0), 2, axis=1), 2, axis=2)


def sweep_padded(values, source_term, face_set, diagonal, level_scale):
    return values + DAMPING * (source_term - apply_padded(values, face_set, level_scale)) / diagonal


def sweep_rimmed(values, source_term, face_set, diagonal, level_scale):
    return values + DAMPING * (source_term - apply_rimmed(values, face_set, level_scale)) / diagonal


def bottom_solve(source_term, face_set, level_scale):
    diagonal = diagonal_of(face_set, level_scale)

    def one_sweep(sweep_index, current):
        return sweep_padded(current, source_term, face_set, diagonal, level_scale)

    return lax.fori_loop(0, BOTTOM, one_sweep, jnp.zeros_like(source_term))


def bottom_level(source_term, face_set):
    face_x, face_y, face_z = face_set
    narrow_count = lax.axis_size("narrow")
    narrow_index = lax.axis_index("narrow")
    weight = (jnp.arange(narrow_count) == narrow_index).astype(jnp.float32)

    def spread(piece):
        placed = weight[:, None, None, None] * piece[None]
        return placed.reshape((narrow_count * piece.shape[0],) + piece.shape[1:])

    last_face = face_x[-1:] * (narrow_index == narrow_count - 1).astype(jnp.float32)
    summed = (
        lax.psum(spread(source_term).astype(jnp.bfloat16), "narrow").astype(jnp.float32),
        lax.psum(spread(face_x[:-1]).astype(jnp.bfloat16), "narrow").astype(jnp.float32),
        lax.psum(spread(face_y).astype(jnp.bfloat16), "narrow").astype(jnp.float32),
        lax.psum(spread(face_z).astype(jnp.bfloat16), "narrow").astype(jnp.float32),
        lax.psum(last_face.astype(jnp.bfloat16), "narrow").astype(jnp.float32),
    )
    group_source, head_x, group_y, group_z, last_faces = summed
    group_x = jnp.concatenate([head_x, last_faces], 0)
    solved = bottom_solve(group_source, (group_x, group_y, group_z), 0.25**LEVELS)
    return lax.dynamic_slice_in_dim(
        solved, narrow_index * source_term.shape[0], source_term.shape[0], 0
    )


def project(solve_local):
    patch_cube = solve_local.reshape(BXP, BYP, BZP, 4, PATCH, PATCH, PATCH)
    grid_fields = jnp.transpose(patch_cube, (3, 0, 4, 1, 5, 2, 6)).reshape(
        4, BXP * PATCH, BYP * PATCH, BZP * PATCH
    )
    rim_fields = padded_2(
        jnp.stack([grid_fields[0], grid_fields[1], grid_fields[3]]), (("wide", 2), ("narrow", 1)), 1
    ).astype(jnp.float32)
    velocity_x = rim_fields[0]
    velocity_y = rim_fields[1]
    density_rim = rim_fields[2]
    velocity_z = grid_fields[2].astype(jnp.float32)
    lower_z, upper_z = neighbours(velocity_z, 2)
    differences = (
        velocity_x[2:, 1:-1] - velocity_x[:-2, 1:-1],
        velocity_y[1:-1, 2:] - velocity_y[1:-1, :-2],
        upper_z - lower_z,
    )
    source_term = -0.5 * (differences[0] + differences[1] + differences[2])
    inner_x = density_rim[:, 1:-1]
    face_x = 2.0 / (inner_x[:-1] + inner_x[1:])
    inner_y = density_rim[1:-1]
    face_y = 2.0 / (inner_y[:, :-1] + inner_y[:, 1:])
    face_z = face_along(density_rim[1:-1, 1:-1], 2)
    face_set = (face_x, face_y, face_z)
    stored = []
    for level_index in range(LEVELS):
        level_scale = 0.25**level_index
        diagonal = diagonal_of(face_set, level_scale)
        values = DAMPING * source_term / diagonal
        values = sweep_rimmed(values, source_term, face_set, diagonal, level_scale)
        residual = source_term - apply_rimmed(values, face_set, level_scale)
        stored.append((values, source_term, face_set, diagonal, level_scale))
        source_term = restrict_mean(residual)
        face_set = coarsen_faces(face_set)
    correction = bottom_level(source_term, face_set)
    for level_index in reversed(range(LEVELS)):
        values, source_term, face_set, diagonal, level_scale = stored[level_index]
        values = values + prolong(correction)
        values = sweep_rimmed(values, source_term, face_set, diagonal, level_scale)
        values = sweep_rimmed(values, source_term, face_set, diagonal, level_scale)
        correction = values
    return correction


def shards(target_slot, fields):
    per_owner = fields.shape[0]
    owners = lax.axis_size("wide") * lax.axis_size("narrow")
    owner_index = lax.axis_index("wide") * lax.axis_size("narrow") + lax.axis_index("narrow")
    capacity = 2 * ((per_owner // 2 + owners - 1) // owners)
    positions = jnp.arange(per_owner, dtype=jnp.int32)
    own_row = lax.dynamic_slice_in_dim(target_slot, owner_index * per_owner, per_owner)
    own_target = own_row // per_owner
    earlier = jnp.sum(
        (
            (own_target[:, None] == own_target[None, :]) & (positions[:, None] > positions[None, :])
        ).astype(jnp.int32),
        axis=1,
    )
    send_index = (
        jnp.full((owners * capacity,), per_owner, jnp.int32)
        .at[own_target * capacity + earlier]
        .set(positions)
    )
    slot_table = target_slot.reshape(owners, per_owner)
    to_owner = (slot_table // per_owner == owner_index).astype(jnp.int32)
    arrival_rank = jnp.cumsum(to_owner, axis=1) - to_owner
    source_rows = jnp.arange(owners, dtype=jnp.int32)[:, None] * capacity + arrival_rank
    arrival = jnp.where(to_owner == 1, slot_table % per_owner, per_owner)
    receive_index = (
        jnp.zeros((per_owner,), jnp.int32)
        .at[arrival.reshape(-1)]
        .set(source_rows.reshape(-1), mode="drop")
    )
    arrived = lax.all_to_all(
        jnp.take(fields, send_index, axis=0, mode="fill", fill_value=0),
        ("wide", "narrow"),
        split_axis=0,
        concat_axis=0,
        tiled=True,
    )
    migrated = jnp.take(arrived, receive_index, axis=0)
    pressure = project(migrated[:, :4])
    return (migrated, pressure)


def solution(mesh):
    in_specs = (P(), P(("wide", "narrow"), None, None))
    out_specs = (P(("wide", "narrow"), None, None), P("narrow", "wide", None))
    return jax.shard_map(shards, mesh=mesh, in_specs=in_specs, out_specs=out_specs, check_vma=False)
```

profile of v0, /device:TPU:1, one launch (start us, length us, event | category | flops | bytes accessed | tf_op | source)
XLA Modules:
  0.0 567.7 jit_solution(10024439724805006023)
XLA Ops:
  6.1 4.5 broadcast_select_fusion.1
  10.6 7.2 %all-to-all-start = ((bf16[64,8,4096]{2,1,0:T(8,128)(2,1)}), bf16[64,8,4096]{2,1,0:T(8,128)(2,1)}, u32[]{:S(2)}, u32[]{:S(2)}) async-start(bf16[64,8,4096]{2,1,0:T(8,128)(2,1)} %broadcast_select_fusion.1), calls=%async_computation | async-start | bytes 8388608 | tf_op jit(solution)/shard_map/all_to_all | solution.py:241
  18.3 4.3 scatter_custom_fusion
  22.7 88.4 %all-to-all-done = bf16[64,8,4096]{2,1,0:T(8,128)(2,1)} async-done(((bf16[64,8,4096]{2,1,0:T(8,128)(2,1)}), bf16[64,8,4096]{2,1,0:T(8,128)(2,1)}, u32[]{:S(2)}, u32[]{:S(2)}) %all-to-all-start) | async-done | bytes 4194336 | tf_op jit(solution)/shard_map/all_to_all | solution.py:241
  116.7 8.4 %reshape.131 = bf16[1,4,8,4,16,16,16]{6,5,4,2,1,3,0:T(8,128)(2,1)} reshape(bf16[32,4,4096]{2,0,1:T(8,128)(2,1)S(1)} %copy.133) | data formatting | bytes 2097152 | tf_op jit(solution)/shard_map/reshape | solution.py:168
  125.1 6.3 %slice_convert_fusion = (f32[1,1,16,4,16,8,16]{6,4,2,5,3,0,1:T(8,128)}, bf16[1,1,16,4,16,8,16]{6,4,2,5,3,0,1:T(8,128)(2,1)S(1)}, bf16[1,1,16,4,16,8,16]{6,4,2,5,...) fusion(bf16[4,1,16,4,16,8,16]{6,4,2,5,3,0,1:T(8,128)(2,1)} %bitcast.52), kind=kLoop, calls=%fused_computation.7 | loop fusion | flops 131072 | bytes 2359296 | tf_op jit(solution)/shard_map/convert_element_type | solution.py:178
  131.4 3.8 copy.134
  138.2 5.4 copy.135
  146.6 3.8 copy.136
  158.6 6.6 %copy.137 = f32[1,1,16,4,16,8,16]{6,5,4,3,2,1,0:T(8,128)} copy(f32[1,1,16,4,16,8,16]{6,4,2,5,3,0,1:T(8,128)} %get-tuple-element.103) | data formatting | bytes 1048576 | tf_op jit(solution)/shard_map/convert_element_type | solution.py:178
  168.5 4.4 collective-permute-start.2
  182.6 9.7 %slice.768 = f32[16,64,65]{2,1,0:T(8,128)} slice(f32[16,64,129]{2,1,0:T(8,128)S(1)} %add_divide_fusion), slice={[0:16:1], [0:64:1], [0:129:2]} | slice | bytes 532480 | tf_op jit(solution)/shard_map/slice | solution.py:108
  193.7 4.8 collective-permute-start.4
  202.9 6.6 %reduce_sum.119 = f32[9,32,64]{0,2,1:T(8,128)} reduce(f32[9,32,2,64,2]{0,4,3,2,1:T(2,128)} %bitcast.53, f32[]{:T(128)} %constant.148.clone.1), dimensions={2,4}, to_apply=%region_5.6 | reduce | flops 55296 | bytes 368644 | tf_op jit(solution)/shard_map/reduce_sum | solution.py:103
  238.4 4.0 collective-permute-start.8
  248.9 4.3 collective-permute-start.11
  255.6 35.7 %reshape.132 = f32[8,2,32,2,64,2]{5,4,3,2,1,0:T(8,128)} reshape(f32[16,64,128]{2,1,0:T(8,128)} %fusion.39) | data formatting | bytes 1048576 | tf_op jit(solution)/shard_map/reshape | solution.py:117
  291.4 12.2 %reduce_sum.118 = f32[8,32,64]{2,1,0:T(8,128)S(1)} reduce(f32[8,2,32,2,64,2]{5,4,3,2,1,0:T(8,128)} %reshape.132, f32[]{:T(128)} %constant.148.clone.1), dimensions={1,3,5}, to_apply=%region_4.5 | reduce | flops 114688 | bytes 589828 | tf_op jit(solution)/shard_map/reduce_sum | solution.py:117
  313.9 5.7 collective-permute-start.15
  331.6 5.6 collective-permute-start.19
  338.9 6.5 %reshape.136 = f32[4,2,16,2,32,2]{5,4,3,2,1,0:T(8,128)} reshape(f32[8,32,64]{2,1,0:T(8,128)} %fusion.106) | data formatting | bytes 131072 | tf_op jit(solution)/shard_map/reshape | solution.py:117
  358.7 5.6 collective-permute-start.23
  378.5 4.5 collective-permute-start.27
  389.1 12.8 %all-reduce.34 = (bf16[1,8,16]{2,1,0:T(8,128)(2,1)}, bf16[8,8,16]{2,1,0:T(8,128)(2,1)}, bf16[8,9,16]{2,1,0:T(8,128)(2,1)}, bf16[8,8,17]{2,1,0:T(8,128)(2,1)S(1)}, bf16[8,8,16]{2,1,0:T(8,128)(2,1)S(1)}) all-reduce(bf16[1,8,16]{2,1,0:T(8,128)(2,1)} %fusion.215, ...), channel_id=1, replica_groups=mesh['wide'=8,'narrow'=4] {'narrow'}, use_global_device_ids=true, to_apply=%region_14.15 | all-reduce | flops 4416 | bytes 17664 | tf_op jit(solution)/shard_map/psum | solution.py:157
  408.2 38.5 %while.11 = (s32[]{:T(128)}, f32[8,8,16]{2,1,0:T(8,128)}, f32[9,8,16]{2,1,0:T(8,128)}, f32[8,8,16]{2,1,0:T(8,128)}, f32[8,9,16]{2,1,0:T(8,128)}, /*index=5*/f32[...) while((s32[]{:T(128)}, f32[8,8,16]{2,1,0:T(8,128)}, ...), condition=%wide.region_22.23_spmd.clone, body=%wide.region_21.22_spmd.clone.sunk | while | flops 24579 | bytes 115312 | solution.py:138
  449.8 4.3 collective-permute-start.28
  467.6 4.5 collective-permute-start.32
  478.7 5.4 collective-permute-start.35
  501.4 5.6 collective-permute-start.39
  518.2 5.6 collective-permute-start.43
  542.8 5.6 collective-permute-start.47
  559.2 5.7 collective-permute-start.51
  (384 shorter events, 267.3 us)
Async XLA Ops:
  10.6 100.5 %all-to-all-start = ((bf16[64,8,4096]{2,1,0:T(8,128)(2,1)}), bf16[64,8,4096]{2,1,0:T(8,128)(2,1)}, u32[]{:S(2)}, u32[]{:S(2)}) async-start(bf16[64,8,4096]{2,1,0:T(8,128)(2,1)} %broadcast_select_fusion.1), calls=%async_computation | async-start | bytes 8388608 | tf_op jit(solution)/shard_map/all_to_all | solution.py:241
  153.7 14.7 %collective-permute-start = (bf16[3,16,1,128]{3,2,1,0:T(2,128)(2,1)S(1)}, bf16[3,16,1,128]{3,2,1,0:T(2,128)(2,1)S(1)}, u32[]{:S(2)}, u32[]{:S(2)}) collective-permute-start(bf16[3,16,1,128]{3,2,1,0:T(2,128)(2,1)S(1)} %get-tuple-element.112), channel_id=1, source_target_pairs={{0,4},{4,8},{8,12},{12,16},{16,20},{20,24},{24,28},{1,5},{5,9},{9,... | collective-permute-start | bytes 36872 | tf_op jit(solution)/shard_map/ppermute | solution.py:24
  156.6 11.9 %collective-permute-start.1 = (bf16[3,16,1,128]{3,2,1,0:T(2,128)(2,1)S(1)}, bf16[3,16,1,128]{3,2,1,0:T(2,128)(2,1)S(1)}, u32[]{:S(2)}, u32[]{:S(2)}) collective-permute-start(bf16[3,16,1,128]{3,2,1,0:T(2,128)(2,1)S(1)} %get-tuple-element.113), channel_id=1, source_target_pairs={{4,0},{8,4},{12,8},{16,12},{20,16},{24,20},{28,24},{5,1},{9,5},{13... | collective-permute-start | bytes 36872 | tf_op jit(solution)/shard_map/ppermute | solution.py:25
  168.5 6.6 %collective-permute-start.2 = (bf16[3,1,66,128]{3,2,1,0:T(8,128)(2,1)S(1)}, bf16[3,1,66,128]{3,2,1,0:T(8,128)(2,1)S(1)}, u32[]{:S(2)}, u32[]{:S(2)}) collective-permute-start(bf16[3,1,66,128]{3,2,1,0:T(8,128)(2,1)S(1)} %get-tuple-element.110), channel_id=1, source_target_pairs={{0,1},{1,2},{2,3},{4,5},{5,6},{6,7},{8,9},{9,10},{10,11},{12,13},{... | collective-permute-start | bytes 152072 | tf_op jit(solution)/shard_map/ppermute | solution.py:24
  193.7 33.0 %collective-permute-start.4 = (f32[16,1,128]{2,1,0:T(1,128)}, f32[16,1,128]{2,1,0:T(1,128)}, u32[]{:S(2)}, u32[]{:S(2)}) collective-permute-start(f32[16,1,128]{2,1,0:T(1,128)} %get-tuple-element.137), channel_id=1, source_target_pairs={{0,4},{4,8},{8,12},{12,16},{16,20},{20,24},{24,28},{1,5},{5,9},{9,... | collective-permute-start | bytes 24584 | tf_op jit(solution)/shard_map/ppermute | solution.py:24
  198.5 28.2 %collective-permute-start.5 = (f32[16,1,128]{2,1,0:T(1,128)}, f32[16,1,128]{2,1,0:T(1,128)}, u32[]{:S(2)}, u32[]{:S(2)}) collective-permute-start(f32[16,1,128]{2,1,0:T(1,128)} %get-tuple-element.136), channel_id=1, source_target_pairs={{4,0},{8,4},{12,8},{16,12},{20,16},{24,20},{28,24},{5,1},{9,5},{13... | collective-permute-start | bytes 24584 | tf_op jit(solution)/shard_map/ppermute | solution.py:25
  227.4 7.8 %collective-permute-start.6 = (f32[1,66,128]{2,1,0:T(8,128)S(1)}, f32[1,66,128]{2,1,0:T(8,128)S(1)}, u32[]{:S(2)}, u32[]{:S(2)}) collective-permute-start(f32[1,66,128]{2,1,0:T(8,128)S(1)} %get-tuple-element.120), channel_id=1, source_target_pairs={{1,0},{2,1},{3,2},{5,4},{6,5},{7,6},{9,8},{10,9},{11,10},{13,12},{... | collective-permute-start | bytes 101384 | tf_op jit(solution)/shard_map/ppermute | solution.py:25
  229.3 5.8 %collective-permute-start.7 = (f32[1,66,128]{2,1,0:T(8,128)S(1)}, f32[1,66,128]{2,1,0:T(8,128)S(1)}, u32[]{:S(2)}, u32[]{:S(2)}) collective-permute-start(f32[1,66,128]{2,1,0:T(8,128)S(1)} %get-tuple-element.121), channel_id=1, source_target_pairs={{0,1},{1,2},{2,3},{4,5},{5,6},{6,7},{8,9},{9,10},{10,11},{12,13},{... | collective-permute-start | bytes 101384 | tf_op jit(solution)/shard_map/ppermute | solution.py:24
  246.8 6.6 %collective-permute-start.10 = (f32[1,66,128]{2,1,0:T(8,128)S(1)}, f32[1,66,128]{2,1,0:T(8,128)S(1)}, u32[]{:S(2)}, u32[]{:S(2)}) collective-permute-start(f32[1,66,128]{2,1,0:T(8,128)S(1)} %get-tuple-element.118), channel_id=1, source_target_pairs={{1,0},{2,1},{3,2},{5,4},{6,5},{7,6},{9,8},{10,9},{11,10},{13,12},{... | collective-permute-start | bytes 101384 | tf_op jit(solution)/shard_map/ppermute | solution.py:25
  303.7 7.8 %collective-permute-start.12 = (f32[8,1,64]{2,1,0:T(1,128)S(1)}, f32[8,1,64]{2,1,0:T(1,128)S(1)}, u32[]{:S(2)}, u32[]{:S(2)}) collective-permute-start(f32[8,1,64]{2,1,0:T(1,128)S(1)} %get-tuple-element.163), channel_id=1, source_target_pairs={{0,4},{4,8},{8,12},{12,16},{16,20},{20,24},{24,28},{1,5},{5,9},{9,... | collective-permute-start | bytes 6152 | tf_op jit(solution)/shard_map/ppermute | solution.py:24
  311.9 7.7 %collective-permute-start.14 = (f32[1,34,64]{2,0,1:T(1,128)S(1)}, f32[1,34,64]{2,0,1:T(1,128)S(1)}, u32[]{:S(2)}, u32[]{:S(2)}) collective-permute-start(f32[1,34,64]{2,0,1:T(1,128)S(1)} %copy.142), channel_id=1, source_target_pairs={{1,0},{2,1},{3,2},{5,4},{6,5},{7,6},{9,8},{10,9},{11,10},{13,12},{... | collective-permute-start | bytes 26120 | tf_op jit(solution)/shard_map/ppermute | solution.py:25
  313.9 6.5 %collective-permute-start.15 = (f32[1,34,64]{2,0,1:T(1,128)S(1)}, f32[1,34,64]{2,0,1:T(1,128)S(1)}, u32[]{:S(2)}, u32[]{:S(2)}) collective-permute-start(f32[1,34,64]{2,0,1:T(1,128)S(1)} %copy.144), channel_id=1, source_target_pairs={{0,1},{1,2},{2,3},{4,5},{5,6},{6,7},{8,9},{9,10},{10,11},{12,13},{... | collective-permute-start | bytes 26120 | tf_op jit(solution)/shard_map/ppermute | solution.py:24
  329.6 7.7 %collective-permute-start.18 = (f32[1,34,64]{2,0,1:T(1,128)S(1)}, f32[1,34,64]{2,0,1:T(1,128)S(1)}, u32[]{:S(2)}, u32[]{:S(2)}) collective-permute-start(f32[1,34,64]{2,0,1:T(1,128)S(1)} %copy.146), channel_id=1, source_target_pairs={{1,0},{2,1},{3,2},{5,4},{6,5},{7,6},{9,8},{10,9},{11,10},{13,12},{... | collective-permute-start | bytes 26120 | tf_op jit(solution)/shard_map/ppermute | solution.py:25
  331.6 6.5 %collective-permute-start.19 = (f32[1,34,64]{2,0,1:T(1,128)S(1)}, f32[1,34,64]{2,0,1:T(1,128)S(1)}, u32[]{:S(2)}, u32[]{:S(2)}) collective-permute-start(f32[1,34,64]{2,0,1:T(1,128)S(1)} %copy.148), channel_id=1, source_target_pairs={{0,1},{1,2},{2,3},{4,5},{5,6},{6,7},{8,9},{9,10},{10,11},{12,13},{... | collective-permute-start | bytes 26120 | tf_op jit(solution)/shard_map/ppermute | solution.py:24
  356.8 7.6 %collective-permute-start.22 = (f32[1,18,32]{2,1,0:T(8,128)S(1)}, f32[1,18,32]{2,1,0:T(8,128)S(1)}, u32[]{:S(2)}, u32[]{:S(2)}) collective-permute-start(f32[1,18,32]{2,1,0:T(8,128)S(1)} %get-tuple-element.170), channel_id=1, source_target_pairs={{1,0},{2,1},{3,2},{5,4},{6,5},{7,6},{9,8},{10,9},{11,10},{13,12},{... | collective-permute-start | bytes 6920 | tf_op jit(solution)/shard_map/ppermute | solution.py:25
  358.7 6.5 %collective-permute-start.23 = (f32[1,18,32]{2,1,0:T(8,128)S(1)}, f32[1,18,32]{2,1,0:T(8,128)S(1)}, u32[]{:S(2)}, u32[]{:S(2)}) collective-permute-start(f32[1,18,32]{2,1,0:T(8,128)S(1)} %get-tuple-element.171), channel_id=1, source_target_pairs={{0,1},{1,2},{2,3},{4,5},{5,6},{6,7},{8,9},{9,10},{10,11},{12,13},{... | collective-permute-start | bytes 6920 | tf_op jit(solution)/shard_map/ppermute | solution.py:24
  366.7 9.2 %collective-permute-start.24 = (f32[4,1,32]{2,1,0:T(1,128)}, f32[4,1,32]{2,1,0:T(1,128)}, u32[]{:S(2)}, u32[]{:S(2)}) collective-permute-start(f32[4,1,32]{2,1,0:T(1,128)} %get-tuple-element.183), channel_id=1, source_target_pairs={{0,4},{4,8},{8,12},{12,16},{16,20},{20,24},{24,28},{1,5},{5,9},{9,... | collective-permute-start | bytes 1544 | tf_op jit(solution)/shard_map/ppermute | solution.py:24
  370.1 5.8 %collective-permute-start.25 = (f32[4,1,32]{2,1,0:T(1,128)}, f32[4,1,32]{2,1,0:T(1,128)}, u32[]{:S(2)}, u32[]{:S(2)}) collective-permute-start(f32[4,1,32]{2,1,0:T(1,128)} %get-tuple-element.182), channel_id=1, source_target_pairs={{4,0},{8,4},{12,8},{16,12},{20,16},{24,20},{28,24},{5,1},{9,5},{13... | collective-permute-start | bytes 1544 | tf_op jit(solution)/shard_map/ppermute | solution.py:25
  376.6 6.5 %collective-permute-start.26 = (f32[1,18,32]{2,1,0:T(8,128)S(1)}, f32[1,18,32]{2,1,0:T(8,128)S(1)}, u32[]{:S(2)}, u32[]{:S(2)}) collective-permute-start(f32[1,18,32]{2,1,0:T(8,128)S(1)} %get-tuple-element.168), channel_id=1, source_target_pairs={{1,0},{2,1},{3,2},{5,4},{6,5},{7,6},{9,8},{10,9},{11,10},{13,12},{... | collective-permute-start | bytes 6920 | tf_op jit(solution)/shard_map/ppermute | solution.py:25
  449.8 5.6 collective-permute-start.28
  459.1 6.8 %collective-permute-start.30 = (f32[1,18,32]{2,1,0:T(8,128)S(1)}, f32[1,18,32]{2,1,0:T(8,128)S(1)}, u32[]{:S(2)}, u32[]{:S(2)}) collective-permute-start(f32[1,18,32]{2,1,0:T(8,128)S(1)} %get-tuple-element.166), channel_id=1, source_target_pairs={{1,0},{2,1},{3,2},{5,4},{6,5},{7,6},{9,8},{10,9},{11,10},{13,12},{... | collective-permute-start | bytes 6920 | tf_op jit(solution)/shard_map/ppermute | solution.py:25
  467.6 5.8 %collective-permute-start.32 = (f32[4,1,32]{2,1,0:T(1,128)S(1)}, f32[4,1,32]{2,1,0:T(1,128)S(1)}, u32[]{:S(2)}, u32[]{:S(2)}) collective-permute-start(f32[4,1,32]{2,1,0:T(1,128)S(1)} %get-tuple-element.175), channel_id=1, source_target_pairs={{0,4},{4,8},{8,12},{12,16},{16,20},{20,24},{24,28},{1,5},{5,9},{9,... | collective-permute-start | bytes 1544 | tf_op jit(solution)/shard_map/ppermute | solution.py:24
  476.5 7.6 %collective-permute-start.34 = (f32[1,18,32]{2,1,0:T(8,128)S(1)}, f32[1,18,32]{2,1,0:T(8,128)S(1)}, u32[]{:S(2)}, u32[]{:S(2)}) collective-permute-start(f32[1,18,32]{2,1,0:T(8,128)S(1)} %get-tuple-element.164), channel_id=1, source_target_pairs={{1,0},{2,1},{3,2},{5,4},{6,5},{7,6},{9,8},{10,9},{11,10},{13,12},{... | collective-permute-start | bytes 6920 | tf_op jit(solution)/shard_map/ppermute | solution.py:25
  478.7 6.2 %collective-permute-start.35 = (f32[1,18,32]{2,1,0:T(8,128)S(1)}, f32[1,18,32]{2,1,0:T(8,128)S(1)}, u32[]{:S(2)}, u32[]{:S(2)}) collective-permute-start(f32[1,18,32]{2,1,0:T(8,128)S(1)} %get-tuple-element.165), channel_id=1, source_target_pairs={{0,1},{1,2},{2,3},{4,5},{5,6},{6,7},{8,9},{9,10},{10,11},{12,13},{... | collective-permute-start | bytes 6920 | tf_op jit(solution)/shard_map/ppermute | solution.py:24
  499.4 7.7 %collective-permute-start.38 = (f32[1,34,64]{2,0,1:T(1,128)S(1)}, f32[1,34,64]{2,0,1:T(1,128)S(1)}, u32[]{:S(2)}, u32[]{:S(2)}) collective-permute-start(f32[1,34,64]{2,0,1:T(1,128)S(1)} %copy.161), channel_id=1, source_target_pairs={{1,0},{2,1},{3,2},{5,4},{6,5},{7,6},{9,8},{10,9},{11,10},{13,12},{... | collective-permute-start | bytes 26120 | tf_op jit(solution)/shard_map/ppermute | solution.py:25
  501.4 6.5 %collective-permute-start.39 = (f32[1,34,64]{2,0,1:T(1,128)S(1)}, f32[1,34,64]{2,0,1:T(1,128)S(1)}, u32[]{:S(2)}, u32[]{:S(2)}) collective-permute-start(f32[1,34,64]{2,0,1:T(1,128)S(1)} %copy.163), channel_id=1, source_target_pairs={{0,1},{1,2},{2,3},{4,5},{5,6},{6,7},{8,9},{9,10},{10,11},{12,13},{... | collective-permute-start | bytes 26120 | tf_op jit(solution)/shard_map/ppermute | solution.py:24
  516.3 7.7 %collective-permute-start.42 = (f32[1,34,64]{2,0,1:T(1,128)S(1)}, f32[1,34,64]{2,0,1:T(1,128)S(1)}, u32[]{:S(2)}, u32[]{:S(2)}) collective-permute-start(f32[1,34,64]{2,0,1:T(1,128)S(1)} %copy.165), channel_id=1, source_target_pairs={{1,0},{2,1},{3,2},{5,4},{6,5},{7,6},{9,8},{10,9},{11,10},{13,12},{... | collective-permute-start | bytes 26120 | tf_op jit(solution)/shard_map/ppermute | solution.py:25
  518.2 6.5 %collective-permute-start.43 = (f32[1,34,64]{2,0,1:T(1,128)S(1)}, f32[1,34,64]{2,0,1:T(1,128)S(1)}, u32[]{:S(2)}, u32[]{:S(2)}) collective-permute-start(f32[1,34,64]{2,0,1:T(1,128)S(1)} %copy.167), channel_id=1, source_target_pairs={{0,1},{1,2},{2,3},{4,5},{5,6},{6,7},{8,9},{9,10},{10,11},{12,13},{... | collective-permute-start | bytes 26120 | tf_op jit(solution)/shard_map/ppermute | solution.py:24
  540.8 7.8 %collective-permute-start.46 = (f32[1,66,128]{2,1,0:T(8,128)S(1)}, f32[1,66,128]{2,1,0:T(8,128)S(1)}, u32[]{:S(2)}, u32[]{:S(2)}) collective-permute-start(f32[1,66,128]{2,1,0:T(8,128)S(1)} %get-tuple-element.116), channel_id=1, source_target_pairs={{1,0},{2,1},{3,2},{5,4},{6,5},{7,6},{9,8},{10,9},{11,10},{13,12},{... | collective-permute-start | bytes 101384 | tf_op jit(solution)/shard_map/ppermute | solution.py:25
  542.8 6.7 %collective-permute-start.47 = (f32[1,66,128]{2,1,0:T(8,128)S(1)}, f32[1,66,128]{2,1,0:T(8,128)S(1)}, u32[]{:S(2)}, u32[]{:S(2)}) collective-permute-start(f32[1,66,128]{2,1,0:T(8,128)S(1)} %get-tuple-element.117), channel_id=1, source_target_pairs={{0,1},{1,2},{2,3},{4,5},{5,6},{6,7},{8,9},{9,10},{10,11},{12,13},{... | collective-permute-start | bytes 101384 | tf_op jit(solution)/shard_map/ppermute | solution.py:24
  557.3 7.8 %collective-permute-start.50 = (f32[1,66,128]{2,1,0:T(8,128)S(1)}, f32[1,66,128]{2,1,0:T(8,128)S(1)}, u32[]{:S(2)}, u32[]{:S(2)}) collective-permute-start(f32[1,66,128]{2,1,0:T(8,128)S(1)} %get-tuple-element.114), channel_id=1, source_target_pairs={{1,0},{2,1},{3,2},{5,4},{6,5},{7,6},{9,8},{10,9},{11,10},{13,12},{... | collective-permute-start | bytes 101384 | tf_op jit(solution)/shard_map/ppermute | solution.py:25
  559.2 6.7 %collective-permute-start.51 = (f32[1,66,128]{2,1,0:T(8,128)S(1)}, f32[1,66,128]{2,1,0:T(8,128)S(1)}, u32[]{:S(2)}, u32[]{:S(2)}) collective-permute-start(f32[1,66,128]{2,1,0:T(8,128)S(1)} %get-tuple-element.115), channel_id=1, source_target_pairs={{0,1},{1,2},{2,3},{4,5},{5,6},{6,7},{8,9},{9,10},{10,11},{12,13},{... | collective-permute-start | bytes 101384 | tf_op jit(solution)/shard_map/ppermute | solution.py:24
  (36 other events, 821.7 us)
where the time goes:
time: 577 us; the launch traced here: 568 us
  starting transfers between devices  161 us (28%)
  local copies, waits for them, and re-layouts  149 us (26%)
  waiting for transfers between devices  127 us (22%)
  other arithmetic  116 us (20%)
  blocking collectives  12.8 us (2%)
    ppermute x26, starting transfers between devices, padded_2(): before = lax.ppermute(last, axis, up)  111 us
    all_to_all x1, waiting for transfers between devices, shards(): lax.all_to_all(jnp.take(fields, send_index, axis=0, mode='fill', fill_val...  88.4 us
    reshape x3, local copies, waits for them, and re-layouts, restrict_mean(): values.reshape(shape[0] // 2, 2, shape[1] // 2, 2, shape[2] // 2, 2)  44.1 us
    ppermute x26, starting transfers between devices, padded_2(): after = lax.ppermute(initial, axis, down)  43.4 us
    ppermute x26, waiting for transfers between devices, padded_2(): after = lax.ppermute(initial, axis, down)  30 us
    add x16, other arithmetic, sweep_padded(): values + DAMPING * (source_term - apply_padded(values, face_set, level_sc...  25.4 us
    reduce_sum x3, other arithmetic, restrict_mean(): values.reshape(shape[0] // 2, 2, shape[1] // 2, 2, shape[2] // 2, 2)  15.9 us
    psum x1, blocking collectives, bottom_level(): lax.psum(last_face.astype(jnp.bfloat16), 'narrow').astype(jnp.float32)  12.8 us
  transfers between devices with their start and end apart: 53, of which 23 were waited for; matrix products, arithmetic and copies ran while one was open for 10% of the time, Pallas kernels for 0%

commit v1 on v0

v1 whole, which is shorter than its diff:
```python
import functools

import jax
import jax.numpy as jnp
from jax import lax
from jax.experimental import pallas as pl
from jax.experimental.pallas import tpu as pltpu
from jax.sharding import PartitionSpec as P

PATCH = 16
BYP = 4
BZP = 8
LEVELS = 3
BOTTOM = 16
DAMPING = 0.8
KEEP = 1.0 - DAMPING
SOLVED = 4
CAPACITY = 2
X0 = PATCH
Y0 = PATCH * BYP
Z = PATCH * BZP
PAD = 8
MESH = pl.DeviceIdType.MESH
VMEM_LIMIT = 60 * 1024 * 1024


def dims(level):
    return X0 >> level, Y0 >> level


def pack_kernel(index_ref, fields_ref, solved_ref, carried_ref):
    def one(slot, carry):
        patch = fields_ref[index_ref[slot]]
        solved_ref[slot] = patch[:SOLVED]
        carried_ref[slot] = patch[SOLVED:]
        return carry

    lax.fori_loop(0, solved_ref.shape[0], one, 0)


def merge_kernel(index_ref, solved_ref, carried_ref, out_ref):
    def one(patch, carry):
        row = index_ref[patch]
        out_ref[patch, :SOLVED] = solved_ref[row]
        out_ref[patch, SOLVED:] = carried_ref[row]
        return carry

    lax.fori_loop(0, out_ref.shape[0], one, 0)


def solve_kernel(
    n_wide,
    n_narrow,
    index_ref,
    arrived_ref,
    out_ref,
    turn,
    tmp,
    grid_u,
    grid_v,
    grid_w,
    grid_r,
    field_sent,
    field_got,
    iterates,
    sent_rows,
    got_rows,
    face_x,
    face_yl,
    face_yh,
    face_zl,
    face_zh,
    diag,
    weight,
    source,
    answer,
    gather_faces,
    gather_source,
    coef,
    send_sem,
    recv_sem,
    gsend_sem,
    grecv_sem,
):
    wide = lax.axis_index("wide")
    narrow = lax.axis_index("narrow")
    has = {
        "xl": narrow > 0,
        "xh": narrow < n_narrow - 1,
        "yl": wide > 0,
        "yh": wide < n_wide - 1,
    }
    peer = {
        "xl": (wide, narrow - 1),
        "xh": (wide, narrow + 1),
        "yl": (wide - 1, narrow),
        "yh": (wide + 1, narrow),
    }
    order = ("xl", "xh", "yl", "yh")
    others = [(wide, lax.rem(narrow + d, n_narrow)) for d in range(1, n_narrow)]

    barrier = pltpu.get_barrier_semaphore()
    beside = [(lax.rem(wide + d, n_wide), narrow) for d in (1, n_wide - 1)]
    for other in others + beside:
        pl.semaphore_signal(barrier, inc=1, device_id=other, device_id_type=MESH)
    pl.semaphore_wait(barrier, len(others) + len(beside))

    lane = lax.broadcasted_iota(jnp.int32, (8, Z), 1)
    block_lane = lane // PATCH

    lower_bits = [(block_lane // s) % 2 == 1 for s in (1, 2, 4)]

    def to_grid(step, carry):
        b = step // X0
        i = step % X0
        at = pl.multiple_of(i * 2 * Z, 2 * Z)
        rows = []
        for c in range(BZP):
            both = arrived_ref[index_ref[b * BZP + c], :, pl.ds(at, 2 * Z)].astype(
                jnp.float32
            )
            rows.append(jnp.concatenate([both[:, :Z], both[:, Z:]], axis=0))
        for bit, s in zip(lower_bits, (1, 2, 4)):
            new = list(rows)
            for c in range(BZP):
                if c & s == 0:
                    low, high = rows[c], rows[c + s]
                    new[c] = jnp.where(bit, pltpu.roll(high, PATCH * s, 1), low)
                    new[c + s] = jnp.where(bit, high, pltpu.roll(low, Z - PATCH * s, 1))
            rows = new
        for j in range(8):
            turn[8 * j : 8 * j + 8, :] = rows[j]
        for half in range(2):
            y = pl.multiple_of(b * PATCH + half * 8, 8)
            for f, ref in enumerate((grid_u, grid_v, grid_w, grid_r)):
                values = turn[pl.ds(half * SOLVED + f, 8, stride=8), :]
                if f == 2:
                    ref[i, pl.ds(y, 8), :] = values
                else:
                    ref[i + 1, pl.ds(PAD + y, 8), :] = values
        return carry

    lax.fori_loop(0, BYP * X0, to_grid, 0)

    def exchange(padded, X, Y, sent, got, slot, sides):
        mid = pl.ds(PAD, Y)
        ends = {
            "xl": (lambda: padded.at[1, mid], lambda: padded.at[X + 1, mid]),
            "xh": (lambda: padded.at[X, mid], lambda: padded.at[0, mid]),
            "yl": (lambda: sent.at[0], lambda: got.at[1]),
            "yh": (lambda: sent.at[1], lambda: got.at[0]),
        }
        back = {"xl": "xh", "xh": "xl", "yl": "yh", "yh": "yl"}

        def copy(side):
            src, dst = ends[side]
            return pltpu.make_async_remote_copy(
                src_ref=src(),
                dst_ref=dst(),
                send_sem=send_sem.at[slot, order.index(side)],
                recv_sem=recv_sem.at[slot, order.index(back[side])],
                device_id=peer[side],
                device_id_type=MESH,
            )

        def landing(side):
            src, dst = ends[back[side]]
            return pltpu.make_async_remote_copy(
                src_ref=src(),
                dst_ref=dst(),
                send_sem=send_sem.at[slot, order.index(side)],
                recv_sem=recv_sem.at[slot, order.index(side)],
                device_id=peer[side],
                device_id_type=MESH,
            )

        def start():
            for side in sides:

                @pl.when(has[side])
                def _():
                    copy(side).start()

        def finish():
            for side in sides:

                @pl.when(has[side])
                def _():
                    landing(side).wait_recv()

                @pl.when(jnp.logical_not(has[side]))
                def _():
                    if side == "xl":
                        padded[0, PAD : PAD + Y, :] = jnp.zeros((Y, Z), jnp.float32)
                    elif side == "xh":
                        padded[X + 1, PAD : PAD + Y, :] = jnp.zeros((Y, Z), jnp.float32)
                    elif side == "yl":
                        got[0] = jnp.zeros((X, Z), jnp.float32)
                    else:
                        got[1] = jnp.zeros((X, Z), jnp.float32)

            if "yl" in sides:

                for x in range(X):
                    padded[x + 1, PAD - 1 : PAD, :] = got[0, x : x + 1, :]
                    padded[x + 1, PAD + Y : PAD + Y + 1, :] = got[1, x : x + 1, :]

        def drain():
            for side in sides:

                @pl.when(has[side])
                def _():
                    copy(side).wait_send()

        return start, finish, drain

    drains = []

    for k, ref in ((0, grid_v), (1, grid_r)):
        for x in range(X0):
            field_sent[k, 0, x : x + 1, :] = ref[x + 1, PAD : PAD + 1, :]
            field_sent[k, 1, x : x + 1, :] = ref[x + 1, PAD + Y0 - 1 : PAD + Y0, :]
    field_moves = [
        exchange(grid_r, X0, Y0, field_sent.at[1], field_got.at[1], 0, order),
        exchange(grid_u, X0, Y0, None, None, 1, ("xl", "xh")),
        exchange(grid_v, X0, Y0, field_sent.at[0], field_got.at[0], 2, ("yl", "yh")),
    ]
    for start, finish, drain in field_moves:
        start()
        drains.append(drain)
    for start, finish, drain in field_moves:
        finish()

    def z_low(values, step):
        rolled = pltpu.roll(values, step, 1)
        at = lax.broadcasted_iota(jnp.int32, values.shape, 1)
        return jnp.where(at < step, 0.0, rolled)

    def z_high(values, step):
        rolled = pltpu.roll(values, Z - step, 1)
        at = lax.broadcasted_iota(jnp.int32, values.shape, 1)
        return jnp.where(at >= Z - step, 0.0, rolled)

    mid0 = pl.ds(PAD, Y0)

    def first(x, carry):
        here = grid_r[x + 1, mid0, :]
        fxl = 2.0 / (grid_r[x, mid0, :] + here)
        fxh = 2.0 / (here + grid_r[x + 2, mid0, :])
        fyl = 2.0 / (grid_r[x + 1, PAD - 1 : PAD - 1 + Y0, :] + here)
        fyh = 2.0 / (grid_r[x + 1, PAD + 1 : PAD + 1 + Y0, :] + here)
        fzl = 2.0 / (z_low(here, 1) + here)
        fzh = 2.0 / (z_high(here, 1) + here)
        face_x[0][x] = fxl
        face_x[0][x + 1] = fxh
        face_yl[0][x] = fyl
        face_yh[0][x] = fyh
        face_zl[0][x] = fzl
        face_zh[0][x] = fzh
        total = ((fxl + fxh) + (fyl + fyh)) + (fzl + fzh)
        diag[0][x] = total
        weight[0][x] = DAMPING / total
        w = grid_w[x]
        du = grid_u[x + 2, mid0, :] - grid_u[x, mid0, :]
        dv = (
            grid_v[x + 1, PAD + 1 : PAD + 1 + Y0, :]
            - grid_v[x + 1, PAD - 1 : PAD - 1 + Y0, :]
        )
        source[0][x] = -0.5 * ((du + dv) + (z_high(w, 1) - z_low(w, 1)))
        return carry

    lax.fori_loop(0, X0, first, 0)

    def z_bit(shape, level):
        at = lax.broadcasted_iota(jnp.int32, shape, 1)
        return (at // (1 << level)) % 2 == 1

    def z_pair(values, level):
        step = 1 << level
        other = jnp.where(
            z_bit(values.shape, level),
            pltpu.roll(values, step, 1),
            pltpu.roll(values, Z - step, 1),
        )
        return values + other

    def z_even(values, level):
        step = 1 << level
        return jnp.where(
            z_bit(values.shape, level), pltpu.roll(values, step, 1), values
        )

    def z_odd(values, level):
        step = 1 << level
        return jnp.where(
            z_bit(values.shape, level), values, pltpu.roll(values, Z - step, 1)
        )

    for level in range(LEVELS):
        X, Y = dims(level + 1)
        even, odd = pl.ds(0, Y, stride=2), pl.ds(1, Y, stride=2)
        last = level + 1 == LEVELS

        def coarse_x(x, level=level, even=even, odd=odd):
            fx = face_x[level]
            return 0.25 * z_pair(fx[2 * x, even, :] + fx[2 * x, odd, :], level)

        def coarse_rest(x, level=level, even=even, odd=odd):
            yl, yh = face_yl[level], face_yh[level]
            zl, zh = face_zl[level], face_zh[level]
            fyl = 0.25 * z_pair(yl[2 * x, even, :] + yl[2 * x + 1, even, :], level)
            fyh = 0.25 * z_pair(yh[2 * x, odd, :] + yh[2 * x + 1, odd, :], level)
            four_l = (zl[2 * x, even, :] + zl[2 * x, odd, :]) + (
                zl[2 * x + 1, even, :] + zl[2 * x + 1, odd, :]
            )
            four_h = (zh[2 * x, even, :] + zh[2 * x, odd, :]) + (
                zh[2 * x + 1, even, :] + zh[2 * x + 1, odd, :]
            )
            return fyl, fyh, z_even(0.25 * four_l, level), z_odd(0.25 * four_h, level)

        if last:
            for x in range(X + 1):
                gather_faces[narrow, x] = coarse_x(x)
            for x in range(X):
                for k, face in enumerate(coarse_rest(x)):
                    gather_faces[narrow, X + 1 + k * X + x] = face
        else:

            def planes(x, carry, level=level, rest=coarse_rest, cx=coarse_x):
                fxl, fxh = cx(x), cx(x + 1)
                fyl, fyh, fzl, fzh = rest(x)
                face_x[level + 1][x] = fxl
                face_x[level + 1][x + 1] = fxh
                face_yl[level + 1][x] = fyl
                face_yh[level + 1][x] = fyh
                face_zl[level + 1][x] = fzl
                face_zh[level + 1][x] = fzh
                total = ((fxl + fxh) + (fyl + fyh)) + (fzl + fzh)
                diag[level + 1][x] = total
                weight[level + 1][x] = DAMPING / total
                return carry

            lax.fori_loop(0, X, planes, 0)

    def gather(ref, which):
        def copy(d):
            return pltpu.make_async_remote_copy(
                src_ref=ref.at[narrow],
                dst_ref=ref.at[narrow],
                send_sem=gsend_sem.at[which, d - 1],
                recv_sem=grecv_sem.at[which, d - 1],
                device_id=others[d - 1],
                device_id_type=MESH,
            )

        def landing(d):
            came = lax.rem(narrow + n_narrow - d, n_narrow)
            return pltpu.make_async_remote_copy(
                src_ref=ref.at[narrow],
                dst_ref=ref.at[came],
                send_sem=gsend_sem.at[which, d - 1],
                recv_sem=grecv_sem.at[which, d - 1],
                device_id=others[d - 1],
                device_id_type=MESH,
            )

        def start():
            for d in range(1, n_narrow):
                copy(d).start()

        def finish():
            for d in range(1, n_narrow):
                landing(d).wait_recv()

        def drain():
            for d in range(1, n_narrow):
                copy(d).wait_send()

        return start, finish, drain

    face_start, face_finish, face_drain = gather(gather_faces, 0)
    source_start, source_finish, source_drain = gather(gather_source, 1)
    face_start()

    def neighbour_sum(level, e, x):
        _, Y = dims(level)
        p = iterates[level]
        step = 1 << level
        mid = pl.ds(PAD, Y)
        here = p[e, x + 1, mid, :]
        total = (
            face_x[level][x] * p[e, x, mid, :]
            + face_x[level][x + 1] * p[e, x + 2, mid, :]
        )
        total += face_yl[level][x] * p[e, x + 1, PAD - 1 : PAD - 1 + Y, :]
        total += face_yh[level][x] * p[e, x + 1, PAD + 1 : PAD + 1 + Y, :]
        total += face_zl[level][x] * z_low(here, step)
        total += face_zh[level][x] * z_high(here, step)
        return here, total

    def sweep(level, e, x):
        here, total = neighbour_sum(level, e, x)
        return KEEP * here + weight[level][x] * (source[level][x] + total)

    def produce(level, e, values_of):
        X, Y = dims(level)
        p = iterates[level]

        def plane(x, carry):
            v = values_of(x)
            p[e, x + 1, PAD : PAD + Y, :] = v
            sent_rows[level][e, 0, pl.ds(x, 1), :] = v[:1]
            sent_rows[level][e, 1, pl.ds(x, 1), :] = v[Y - 1 :]
            return carry

        lax.fori_loop(0, X, plane, 0)
        start, finish, drain = exchange(
            p.at[e],
            X,
            Y,
            sent_rows[level].at[e],
            got_rows[level].at[e],
            3 + 4 * level + e,
            order,
        )
        start()
        drains.append(drain)
        finish()

    for level in range(LEVELS):
        X, Y = dims(level)
        produce(level, 0, lambda x, level=level: weight[level][x] * source[level][x])
        produce(level, 1, lambda x, level=level: sweep(level, 0, x))

        def restrict(x, carry, level=level, Y=Y):
            both = None
            for k in range(2):
                here, total = neighbour_sum(level, 1, 2 * x + k)
                left = (source[level][2 * x + k] - diag[level][2 * x + k] * here) + total
                both = left if both is None else both + left
            tmp[:Y, :] = both
            half = Y // 2
            summed = (
                tmp[pl.ds(0, half, stride=2), :] + tmp[pl.ds(1, half, stride=2), :]
            )
            summed = 0.5 * z_pair(summed, level)
            if level + 1 == LEVELS:
                gather_source[narrow, x] = summed
            else:
                source[level + 1][x] = summed
            return carry

        if level + 1 == LEVELS:
            for x in range(X // 2):
                restrict(x, 0)
        else:
            lax.fori_loop(0, X // 2, restrict, 0)

    source_start()
    face_finish()
    source_finish()
    X, Y = dims(LEVELS)
    step = 1 << LEVELS
    row = lax.broadcasted_iota(jnp.int32, (Y, Z), 0)
    col = lax.broadcasted_iota(jnp.int32, (Y, Z), 1)
    for n in range(n_narrow):
        for x in range(X):
            fxl, fxh = gather_faces[n, x], gather_faces[n, x + 1]
            fyl, fyh, fzl, fzh = (gather_faces[n, X + 1 + k * X + x] for k in range(4))
            total = ((fxl + fxh) + (fyl + fyh)) + (fzl + fzh)
            w = DAMPING / total
            at = n * X + x
            coef[0, at] = w * fxl
            coef[1, at] = w * fxh
            coef[2, at] = jnp.where(row == 0, 0.0, w * fyl)
            coef[3, at] = jnp.where(row == Y - 1, 0.0, w * fyh)
            coef[4, at] = jnp.where(col < step, 0.0, w * fzl)
            coef[5, at] = jnp.where(col >= Z - step, 0.0, w * fzh)
            coef[6, at] = w * gather_source[n, x]

    zero_plane = jnp.zeros((1, Y, Z), jnp.float32)

    def bottom(k, cur):
        new = KEEP * cur + coef[6]
        new += coef[0] * jnp.concatenate([zero_plane, cur[:-1]], axis=0)
        new += coef[1] * jnp.concatenate([cur[1:], zero_plane], axis=0)
        new += coef[2] * pltpu.roll(cur, 1, 1)
        new += coef[3] * pltpu.roll(cur, Y - 1, 1)
        new += coef[4] * pltpu.roll(cur, step, 2)
        new += coef[5] * pltpu.roll(cur, Z - step, 2)
        return new

    coef[7] = lax.fori_loop(0, BOTTOM - 1, bottom, coef[6])
    for x in range(X):
        answer[LEVELS][x] = coef[7, narrow * X + x]

    for level in reversed(range(LEVELS)):
        X, Y = dims(level)
        half = Y // 2

        def raised(x, level=level, Y=Y, half=half):
            e = answer[level + 1][x // 2]
            tmp[pl.ds(0, half, stride=2), :] = e
            tmp[pl.ds(1, half, stride=2), :] = e
            return iterates[level][1, x + 1, PAD : PAD + Y, :] + tmp[:Y, :]

        produce(level, 2, raised)
        produce(level, 3, lambda x, level=level: sweep(level, 2, x))
        target = out_ref if level == 0 else answer[level]

        def close(x, carry, level=level, target=target):
            target[x] = sweep(level, 3, x)
            return carry

        lax.fori_loop(0, X, close, 0)

    face_drain()
    source_drain()
    for drain in drains:
        drain()


def f32(*shape):
    return pltpu.VMEM(shape, jnp.float32)


def call_solve(n_wide, n_narrow, receive_index, arrived):
    X3, Y3 = dims(LEVELS)
    levels = [dims(level) for level in range(LEVELS)]
    padded = f32(X0 + 2, Y0 + 2 * PAD, Z)
    each = [f32(X, Y, Z) for X, Y in levels]
    moves = 3 + 4 * LEVELS
    scratch = [
        f32(64, Z),
        f32(Y0, Z),
        padded,
        padded,
        f32(X0, Y0, Z),
        padded,
        f32(2, 2, X0, Z),
        f32(2, 2, X0, Z),
        [f32(4, X + 2, Y + 2 * PAD, Z) for X, Y in levels],
        [f32(4, 2, X, Z) for X, Y in levels],
        [f32(4, 2, X, Z) for X, Y in levels],
        [f32(X + 1, Y, Z) for X, Y in levels],
        each,
        each,
        each,
        each,
        each,
        each,
        each,
        [f32(*dims(level), Z) for level in range(LEVELS + 1)],
        f32(n_narrow, 5 * X3 + 1, Y3, Z),
        f32(n_narrow, X3, Y3, Z),
        f32(8, n_narrow * X3, Y3, Z),
        pltpu.SemaphoreType.DMA((moves, 4)),
        pltpu.SemaphoreType.DMA((moves, 4)),
        pltpu.SemaphoreType.DMA((2, n_narrow - 1)),
        pltpu.SemaphoreType.DMA((2, n_narrow - 1)),
    ]
    return pl.pallas_call(
        functools.partial(solve_kernel, n_wide, n_narrow),
        out_shape=jax.ShapeDtypeStruct((X0, Y0, Z), jnp.float32),
        in_specs=[
            pl.BlockSpec(memory_space=pltpu.SMEM),
            pl.BlockSpec(memory_space=pltpu.VMEM),
        ],
        out_specs=pl.BlockSpec(memory_space=pltpu.VMEM),
        scratch_shapes=scratch,
        compiler_params=pltpu.CompilerParams(
            collective_id=0, has_side_effects=True, vmem_limit_bytes=VMEM_LIMIT
        ),
        cost_estimate=pl.CostEstimate(
            flops=200_000_000, bytes_accessed=200_000_000, transcendentals=0
        ),
    )(receive_index, arrived)


def shards(n_wide, n_narrow, target_slot, fields):
    per_owner, n_fields, cells = fields.shape
    owners = n_wide * n_narrow
    me = lax.axis_index("wide") * n_narrow + lax.axis_index("narrow")
    slots = owners * CAPACITY
    place = jnp.arange(per_owner, dtype=jnp.int32)
    own_target = lax.dynamic_slice_in_dim(target_slot, me * per_owner, per_owner) // per_owner
    earlier = jnp.sum(
        (
            (own_target[:, None] == own_target[None, :]) & (place[:, None] > place[None, :])
        ).astype(jnp.int32),
        axis=1,
    )
    own_slot = own_target * CAPACITY + earlier
    slot_ids = jnp.arange(slots, dtype=jnp.int32)
    send_index = jnp.sum(
        jnp.where(own_slot[None, :] == slot_ids[:, None], place[None, :], 0), axis=1
    )
    table = target_slot.reshape(owners, per_owner)
    to_me = table // per_owner == me
    rank = jnp.sum(
        (to_me[:, None, :] & (place[None, :, None] > place[None, None, :])).astype(jnp.int32),
        axis=2,
    )
    row = jnp.arange(owners, dtype=jnp.int32)[:, None] * CAPACITY + rank
    receive_index = jnp.sum(
        jnp.where(
            target_slot[None, :] == (me * per_owner + place)[:, None], row.reshape(-1)[None, :], 0
        ),
        axis=1,
    )

    smem = pl.BlockSpec(memory_space=pltpu.SMEM)
    vmem = pl.BlockSpec(memory_space=pltpu.VMEM)
    params = pltpu.CompilerParams(vmem_limit_bytes=VMEM_LIMIT)
    carried_fields = n_fields - SOLVED
    solved, carried = pl.pallas_call(
        pack_kernel,
        out_shape=(
            jax.ShapeDtypeStruct((slots, SOLVED, cells), fields.dtype),
            jax.ShapeDtypeStruct((slots, carried_fields, cells), fields.dtype),
        ),
        in_specs=[smem, vmem],
        out_specs=(vmem, vmem),
        compiler_params=params,
    )(send_index, fields)
    swap = functools.partial(
        lax.all_to_all,
        axis_name=("wide", "narrow"),
        split_axis=0,
        concat_axis=0,
        tiled=True,
    )
    solved = swap(solved)
    solved, carried = lax.optimization_barrier((solved, carried))
    carried = swap(carried)
    pressure = call_solve(n_wide, n_narrow, receive_index, solved)
    migrated = pl.pallas_call(
        merge_kernel,
        out_shape=jax.ShapeDtypeStruct(fields.shape, fields.dtype),
        in_specs=[smem, vmem, vmem],
        out_specs=vmem,
        compiler_params=params,
    )(receive_index, solved, carried)
    return migrated, pressure


def solution(mesh):
    body = functools.partial(shards, mesh.shape["wide"], mesh.shape["narrow"])
    in_specs = (P(), P(("wide", "narrow"), None, None))
    out_specs = (P(("wide", "narrow"), None, None), P("narrow", "wide", None))
    return jax.shard_map(body, mesh=mesh, in_specs=in_specs, out_specs=out_specs, check_vma=False)
```

time: 577 us -> 179 us (0.31); the launches traced: 568 us -> 177 us
  starting transfers between devices: 161 us -> 4.57 us
  local copies, waits for them, and re-layouts: 149 us -> 2.23 us
  waiting for transfers between devices: 127 us -> 0.01 us
  other arithmetic: 116 us -> 3.75 us
  Pallas kernels: 0 us -> 111 us
  blocking collectives: 12.8 us -> 55 us
    ppermute x52 -> x0, starting transfers between devices: 154 us -> none  [the longest x26 111 us: padded_2(): before = lax.ppermute(last, axis, up)]
    pallas_call x0 -> x3, Pallas kernels: none -> 111 us  [the longest x1 103 us: call_solve(): pl.pallas_call(functools.partial(solve_kernel, n_wide, n_narrow), out_sha...]
    all_to_all x1, waiting for transfers between devices: 88.4 us -> 0.01 us  [shards(): carried = swap(carried)]
    reshape x12 -> x1, local copies, waits for them, and re-layouts: 62.5 us -> 0.07 us  [shards(): table = target_slot.reshape(owners, per_owner)]
    all_to_all x0 -> x1, blocking collectives: none -> 55 us  [shards(): solved = swap(solved)]
    slice x107 -> x0, local copies, waits for them, and re-layouts: 51.3 us -> none  [the longest x3 11.2 us: coarsen_faces(): picked = face_z[:, :, ::2]]
    ppermute x52 -> x0, waiting for transfers between devices: 38.4 us -> none  [the longest x26 30 us: padded_2(): after = lax.ppermute(initial, axis, down)]
    add x29 -> x3, other arithmetic: 38.4 us -> 0.85 us  [the longest x1 0.77 us: shards(): own_slot = own_target * CAPACITY + earlier]
  transfers between devices with their start and end apart: 53 -> 1, of which waited for: 23 -> 0; matrix products, arithmetic and copies ran while one was open for 10% -> 1% of each run, Pallas kernels for 0% -> 58%
where the time goes in v1:
time: 179 us; the launch traced here: 177 us
  Pallas kernels  111 us (62%)
  blocking collectives  55 us (31%)
  starting transfers between devices  4.57 us (3%)
  other arithmetic  3.75 us (2%)
  local copies, waits for them, and re-layouts  2.23 us (1%)
    pallas_call x1, Pallas kernels, call_solve(): pl.pallas_call(functools.partial(solve_kernel, n_wide, n_narrow), out_sha...  103 us
    all_to_all x1, blocking collectives, shards(): solved = swap(solved)  55 us
    all_to_all x1, starting transfers between devices, shards(): carried = swap(carried)  4.57 us
    pallas_call x1, Pallas kernels, shards(): pl.pallas_call(pack_kernel, out_shape=(jax.ShapeDtypeStruct((slots, SOLVE...  4.36 us
    pallas_call x1, Pallas kernels, shards(): pl.pallas_call(merge_kernel, out_shape=jax.ShapeDtypeStruct(fields.shape,...  4.24 us
  transfers between devices with their start and end apart: 1, of which 0 were waited for; matrix products, arithmetic and copies ran while one was open for 1% of the time, Pallas kernels for 58%

profile of v1, /device:TPU:1, one launch (start us, length us, event | category | flops | bytes accessed | tf_op | source)
XLA Modules:
  0.0 177.5 jit_solution(10514064591728828899)
XLA Ops:
  0.6 0.8 and_select_fusion
  1.4 0.2 convert_reduce_fusion.1
  1.6 0.8 multiply_add_fusion
  2.4 0.6 select_reduce_fusion.1.index_ref
  3.0 4.4 %shard_map.41 = (bf16[64,4,4096]{2,1,0:T(4,128)(2,1)}, bf16[64,4,4096]{2,1,0:T(4,128)(2,1)}) custom-call(s32[64]{0:T(128)} %select_reduce_fusion.1.index_ref, bf16[32,8,4096]{2,1,0:T(8,128)(2,1)} %fields_ref.1), custom_call_target="tpu_custom_call" | custom-call | tf_op jit(solution)/shard_map/pallas_call | solution.py:616
  7.3 55.0 %all_to_all.10.solved_ref.arrived_ref = bf16[64,4,4096]{2,1,0:T(4,128)(2,1)} all-to-all(bf16[64,4,4096]{2,1,0:T(4,128)(2,1)} %get-tuple-element.6), channel_id=1, replica_groups=mesh['wide'=8,'narrow'=4] {'wide','narrow'}, dimensions={0} | all-to-all | bytes 4194304 | tf_op jit(solution)/shard_map/all_to_all | solution.py:633
  62.3 0.0 copy-start.2
  62.3 4.6 %all-to-all-start.1 = ((bf16[64,4,4096]{2,1,0:T(4,128)(2,1)}), bf16[64,4,4096]{2,1,0:T(4,128)(2,1)S(1)}, u32[]{:S(2)}, u32[]{:S(2)}) async-start(bf16[64,4,4096]{2,1,0:T(4,128)(2,1)} %get-tuple-element.9), calls=%async_computation.1 | async-start | bytes 4194304 | tf_op jit(solution)/shard_map/all_to_all | solution.py:635
  66.9 0.0 copy-done.2
  66.9 0.1 reshape.76
  67.0 0.6 convert_reduce_fusion
  67.6 0.1 broadcast_add_fusion
  67.7 0.1 add.45
  67.8 0.7 select_reduce_fusion.index_ref
  68.5 102.6 %shard_map.43 = f32[16,64,128]{2,1,0:T(8,128)} custom-call(s32[32]{0:T(128)} %select_reduce_fusion.index_ref, bf16[64,4,4096]{2,1,0:T(4,128)(2,1)} %all_to_all.10.solved_ref.arrived_ref), custom_call_target="tpu_custom_call" | custom-call | flops 200000000 | bytes 200000000 | tf_op jit(solution)/shard_map/pallas_call | solution.py:562
  171.1 0.0 copy-start.1
  171.1 0.0 all-to-all-done.1.carried_ref
  171.2 0.0 copy-start
  171.2 1.3 copy-done
  172.4 4.2 %shard_map.42 = bf16[32,8,4096]{2,1,0:T(8,128)(2,1)} custom-call(s32[32]{0:T(128)} %select_reduce_fusion.index_ref, bf16[64,4,4096]{2,1,0:T(4,128)(2,1)} %all_to_all.10.solved_ref.arrived_ref, bf16[64,4,4096]{2,1,0:T(4,128)(2,1)} %copy-done), custom_call_target="tpu_custom_call" | custom-call | tf_op jit(solution)/shard_map/pallas_call | solution.py:637
  176.7 0.0 copy-done.1
  176.7 0.8 copy.5
  (3 shorter events, 0.0 us)
Async XLA Ops:
  62.3 4.6 %copy-start.2 = (s32[1024]{0:T(1024)S(1)}, s32[1024]{0:T(1024)}, u32[]{:S(2)}) copy-start(s32[1024]{0:T(1024)} %param.2) | copy-start | bytes 12292
  62.3 108.8 %all-to-all-start.1 = ((bf16[64,4,4096]{2,1,0:T(4,128)(2,1)}), bf16[64,4,4096]{2,1,0:T(4,128)(2,1)S(1)}, u32[]{:S(2)}, u32[]{:S(2)}) async-start(bf16[64,4,4096]{2,1,0:T(4,128)(2,1)} %get-tuple-element.9), calls=%async_computation.1 | async-start | bytes 4194304 | tf_op jit(solution)/shard_map/all_to_all | solution.py:635
  171.1 5.6 %copy-start.1 = (f32[16,64,128]{2,1,0:T(8,128)S(1)}, f32[16,64,128]{2,1,0:T(8,128)}, u32[]{:S(2)}) copy-start(f32[16,64,128]{2,1,0:T(8,128)} %shard_map.43) | copy-start | bytes 1572868
  171.2 1.3 copy-start

commit v2 on v1

--- a/solution.py
+++ b/solution.py
@@ -35,7 +35,7 @@
         carried_ref[slot] = patch[SOLVED:]
         return carry
 
-    lax.fori_loop(0, solved_ref.shape[0], one, 0)
+    lax.fori_loop(0, solved_ref.shape[0], one, 0, unroll=4)
 
 
 def merge_kernel(index_ref, solved_ref, carried_ref, out_ref):
@@ -45,7 +45,7 @@
         out_ref[patch, SOLVED:] = carried_ref[row]
         return carry
 
-    lax.fori_loop(0, out_ref.shape[0], one, 0)
+    lax.fori_loop(0, out_ref.shape[0], one, 0, unroll=4)
 
 
 def solve_kernel(
@@ -140,7 +140,7 @@
                     ref[i + 1, pl.ds(PAD + y, 8), :] = values
         return carry
 
-    lax.fori_loop(0, BYP * X0, to_grid, 0)
+    lax.fori_loop(0, BYP * X0, to_grid, 0, unroll=4)
 
     def exchange(padded, X, Y, sent, got, slot, sides):
         mid = pl.ds(PAD, Y)
@@ -269,7 +269,7 @@
         source[0][x] = -0.5 * ((du + dv) + (z_high(w, 1) - z_low(w, 1)))
         return carry
 
-    lax.fori_loop(0, X0, first, 0)
+    lax.fori_loop(0, X0, first, 0, unroll=4)
 
     def z_bit(shape, level):
         at = lax.broadcasted_iota(jnp.int32, shape, 1)
@@ -340,7 +340,7 @@
                 weight[level + 1][x] = DAMPING / total
                 return carry
 
-            lax.fori_loop(0, X, planes, 0)
+            lax.fori_loop(0, X, planes, 0, unroll=4)
 
     def gather(ref, which):
         def copy(d):
@@ -413,7 +413,7 @@
             sent_rows[level][e, 1, pl.ds(x, 1), :] = v[Y - 1 :]
             return carry
 
-        lax.fori_loop(0, X, plane, 0)
+        lax.fori_loop(0, X, plane, 0, unroll=4)
         start, finish, drain = exchange(
             p.at[e],
             X,
@@ -454,7 +454,7 @@
             for x in range(X // 2):
                 restrict(x, 0)
         else:
-            lax.fori_loop(0, X // 2, restrict, 0)
+            lax.fori_loop(0, X // 2, restrict, 0, unroll=4)
 
     source_start()
     face_finish()
@@ -490,7 +490,7 @@
         new += coef[5] * pltpu.roll(cur, Z - step, 2)
         return new
 
-    coef[7] = lax.fori_loop(0, BOTTOM - 1, bottom, coef[6])
+    coef[7] = lax.fori_loop(0, BOTTOM - 1, bottom, coef[6], unroll=3)
     for x in range(X):
         answer[LEVELS][x] = coef[7, narrow * X + x]
 
@@ -512,7 +512,7 @@
             target[x] = sweep(level, 3, x)
             return carry
 
-        lax.fori_loop(0, X, close, 0)
+        lax.fori_loop(0, X, close, 0, unroll=4)
 
     face_drain()
     source_drain()

time: 179 us -> 172 us (0.961)
  Pallas kernels: 111 us -> 103 us
    pallas_call x1, Pallas kernels: 103 us -> 95 us  [call_solve(): pl.pallas_call(functools.partial(solve_kernel, n_wide, n_narrow), out_sha...]
  transfers between devices with their start and end apart: 1 -> 1, of which waited for: 0 -> 0; matrix products, arithmetic and copies ran while one was open for 1% -> 1% of each run, Pallas kernels for 58% -> 56%
where the time goes in v2:
time: 172 us; the launch traced here: 170 us
  Pallas kernels  103 us (60%)
  blocking collectives  55 us (32%)
  starting transfers between devices  4.57 us (3%)
  other arithmetic  3.75 us (2%)
  local copies, waits for them, and re-layouts  2.23 us (1%)
    pallas_call x1, Pallas kernels, call_solve(): pl.pallas_call(functools.partial(solve_kernel, n_wide, n_narrow), out_sha...  95 us
    all_to_all x1, blocking collectives, shards(): solved = swap(solved)  55 us
    all_to_all x1, starting transfers between devices, shards(): carried = swap(carried)  4.57 us
    pallas_call x1, Pallas kernels, shards(): pl.pallas_call(merge_kernel, out_shape=jax.ShapeDtypeStruct(fields.shape,...  4.13 us
    pallas_call x1, Pallas kernels, shards(): pl.pallas_call(pack_kernel, out_shape=(jax.ShapeDtypeStruct((slots, SOLVE...  4.08 us
  transfers between devices with their start and end apart: 1, of which 0 were waited for; matrix products, arithmetic and copies ran while one was open for 1% of the time, Pallas kernels for 56%

profile of v2, /device:TPU:1, one launch (start us, length us, event | category | flops | bytes accessed | tf_op | source)
XLA Modules:
  0.0 169.5 jit_solution(3731732396945611226)
XLA Ops:
  0.6 0.8 and_select_fusion
  1.4 0.2 convert_reduce_fusion.1
  1.6 0.8 multiply_add_fusion
  2.4 0.6 select_reduce_fusion.1.index_ref
  3.0 4.1 %shard_map.41 = (bf16[64,4,4096]{2,1,0:T(4,128)(2,1)}, bf16[64,4,4096]{2,1,0:T(4,128)(2,1)}) custom-call(s32[64]{0:T(128)} %select_reduce_fusion.1.index_ref, bf16[32,8,4096]{2,1,0:T(8,128)(2,1)} %fields_ref.1), custom_call_target="tpu_custom_call" | custom-call | tf_op jit(solution)/shard_map/pallas_call | solution.py:616
  7.0 55.0 %all_to_all.10.solved_ref.arrived_ref = bf16[64,4,4096]{2,1,0:T(4,128)(2,1)} all-to-all(bf16[64,4,4096]{2,1,0:T(4,128)(2,1)} %get-tuple-element.6), channel_id=1, replica_groups=mesh['wide'=8,'narrow'=4] {'wide','narrow'}, dimensions={0} | all-to-all | bytes 4194304 | tf_op jit(solution)/shard_map/all_to_all | solution.py:633
  62.1 0.0 copy-start.2
  62.1 4.6 %all-to-all-start.1 = ((bf16[64,4,4096]{2,1,0:T(4,128)(2,1)}), bf16[64,4,4096]{2,1,0:T(4,128)(2,1)S(1)}, u32[]{:S(2)}, u32[]{:S(2)}) async-start(bf16[64,4,4096]{2,1,0:T(4,128)(2,1)} %get-tuple-element.9), calls=%async_computation.1 | async-start | bytes 4194304 | tf_op jit(solution)/shard_map/all_to_all | solution.py:635
  66.6 0.0 copy-done.2
  66.6 0.1 reshape.76
  66.7 0.6 convert_reduce_fusion
  67.4 0.1 broadcast_add_fusion
  67.4 0.1 add.45
  67.5 0.7 select_reduce_fusion.index_ref
  68.2 95.0 %shard_map.43 = f32[16,64,128]{2,1,0:T(8,128)} custom-call(s32[32]{0:T(128)} %select_reduce_fusion.index_ref, bf16[64,4,4096]{2,1,0:T(4,128)(2,1)} %all_to_all.10.solved_ref.arrived_ref), custom_call_target="tpu_custom_call" | custom-call | flops 200000000 | bytes 200000000 | tf_op jit(solution)/shard_map/pallas_call | solution.py:562
  163.3 0.0 copy-start.1
  163.3 0.0 all-to-all-done.1.carried_ref
  163.3 0.0 copy-start
  163.3 1.3 copy-done
  164.6 4.1 %shard_map.42 = bf16[32,8,4096]{2,1,0:T(8,128)(2,1)} custom-call(s32[32]{0:T(128)} %select_reduce_fusion.index_ref, bf16[64,4,4096]{2,1,0:T(4,128)(2,1)} %all_to_all.10.solved_ref.arrived_ref, bf16[64,4,4096]{2,1,0:T(4,128)(2,1)} %copy-done), custom_call_target="tpu_custom_call" | custom-call | tf_op jit(solution)/shard_map/pallas_call | solution.py:637
  168.7 0.0 copy-done.1
  168.7 0.8 copy.5
  (3 shorter events, 0.0 us)
Async XLA Ops:
  62.1 4.6 %copy-start.2 = (s32[1024]{0:T(1024)S(1)}, s32[1024]{0:T(1024)}, u32[]{:S(2)}) copy-start(s32[1024]{0:T(1024)} %param.2) | copy-start | bytes 12292
  62.1 101.2 %all-to-all-start.1 = ((bf16[64,4,4096]{2,1,0:T(4,128)(2,1)}), bf16[64,4,4096]{2,1,0:T(4,128)(2,1)S(1)}, u32[]{:S(2)}, u32[]{:S(2)}) async-start(bf16[64,4,4096]{2,1,0:T(4,128)(2,1)} %get-tuple-element.9), calls=%async_computation.1 | async-start | bytes 4194304 | tf_op jit(solution)/shard_map/all_to_all | solution.py:635
  163.3 5.4 %copy-start.1 = (f32[16,64,128]{2,1,0:T(8,128)S(1)}, f32[16,64,128]{2,1,0:T(8,128)}, u32[]{:S(2)}) copy-start(f32[16,64,128]{2,1,0:T(8,128)} %shard_map.43) | copy-start | bytes 1572868
  163.3 1.3 copy-start

commit v3 on v2

--- a/solution.py
+++ b/solution.py
@@ -21,6 +21,8 @@
 Z = PATCH * BZP
 PAD = 8
 MESH = pl.DeviceIdType.MESH
+STRIDE = 13
+SHARES = (4,) + (2,) * 14
 VMEM_LIMIT = 60 * 1024 * 1024
 
 
@@ -53,7 +55,9 @@
     n_narrow,
     index_ref,
     arrived_ref,
+    carried_ref,
     out_ref,
+    moved_ref,
     turn,
     tmp,
     grid_u,
@@ -81,6 +85,9 @@
     recv_sem,
     gsend_sem,
     grecv_sem,
+    carry_send_sem,
+    carry_recv_sem,
+    own_sem,
 ):
     wide = lax.axis_index("wide")
     narrow = lax.axis_index("narrow")
@@ -100,10 +107,70 @@
     others = [(wide, lax.rem(narrow + d, n_narrow)) for d in range(1, n_narrow)]
 
     barrier = pltpu.get_barrier_semaphore()
-    beside = [(lax.rem(wide + d, n_wide), narrow) for d in (1, n_wide - 1)]
-    for other in others + beside:
-        pl.semaphore_signal(barrier, inc=1, device_id=other, device_id_type=MESH)
-    pl.semaphore_wait(barrier, len(others) + len(beside))
+    owners = n_wide * n_narrow
+    me = wide * n_narrow + narrow
+
+    def owner_at(distance):
+        owner = lax.rem(me + distance, owners)
+        return owner, (owner // n_narrow, lax.rem(owner, n_narrow))
+
+    def greet(d, carry):
+        _, device = owner_at(d)
+        pl.semaphore_signal(barrier, inc=1, device_id=device, device_id_type=MESH)
+        return carry
+
+    lax.fori_loop(1, owners, greet, 0)
+    pl.semaphore_wait(barrier, owners - 1)
+
+    def block(owner):
+        return pl.ds(owner * CAPACITY, CAPACITY)
+
+    def carry_copy(k):
+        d = lax.rem(k * STRIDE, owners)
+        owner, device = owner_at(d)
+        return pltpu.make_async_remote_copy(
+            src_ref=carried_ref.at[block(owner)],
+            dst_ref=moved_ref.at[block(me)],
+            send_sem=carry_send_sem.at[k],
+            recv_sem=carry_recv_sem.at[k],
+            device_id=device,
+            device_id_type=MESH,
+        )
+
+    def carry_landing(k):
+        d = lax.rem(k * STRIDE, owners)
+        _, device = owner_at(d)
+        came, _ = owner_at(owners - d)
+        return pltpu.make_async_remote_copy(
+            src_ref=carried_ref.at[block(me)],
+            dst_ref=moved_ref.at[block(came)],
+            send_sem=carry_send_sem.at[k],
+            recv_sem=carry_recv_sem.at[k],
+            device_id=device,
+            device_id_type=MESH,
+        )
+
+    own_copy = pltpu.make_async_copy(
+        carried_ref.at[block(me)], moved_ref.at[block(me)], own_sem
+    )
+    own_copy.start()
+    shares = SHARES
+    bounds = [
+        1 + (owners - 1) * sum(shares[:k]) // sum(shares) for k in range(len(shares) + 1)
+    ]
+    pushed = []
+
+    def push():
+        turn_now = len(pushed)
+        pushed.append(turn_now)
+
+        def begin(k, carry):
+            carry_copy(k).start()
+            return carry
+
+        lax.fori_loop(bounds[turn_now], bounds[turn_now + 1], begin, 0)
+
+    push()
 
     lane = lax.broadcasted_iota(jnp.int32, (8, Z), 1)
     block_lane = lane // PATCH
@@ -228,6 +295,7 @@
     for start, finish, drain in field_moves:
         start()
         drains.append(drain)
+    push()
     for start, finish, drain in field_moves:
         finish()
 
@@ -425,6 +493,7 @@
         )
         start()
         drains.append(drain)
+        push()
         finish()
 
     for level in range(LEVELS):
@@ -457,6 +526,7 @@
             lax.fori_loop(0, X // 2, restrict, 0, unroll=4)
 
     source_start()
+    push()
     face_finish()
     source_finish()
     X, Y = dims(LEVELS)
@@ -514,6 +584,15 @@
 
         lax.fori_loop(0, X, close, 0, unroll=4)
 
+    assert len(pushed) == len(shares)
+
+    def end(k, carry):
+        carry_landing(k).wait_recv()
+        carry_copy(k).wait_send()
+        return carry
+
+    lax.fori_loop(1, owners, end, 0)
+    own_copy.wait()
     face_drain()
     source_drain()
     for drain in drains:
@@ -524,7 +603,7 @@
     return pltpu.VMEM(shape, jnp.float32)
 
 
-def call_solve(n_wide, n_narrow, receive_index, arrived):
+def call_solve(n_wide, n_narrow, receive_index, arrived, carried):
     X3, Y3 = dims(LEVELS)
     levels = [dims(level) for level in range(LEVELS)]
     padded = f32(X0 + 2, Y0 + 2 * PAD, Z)
@@ -558,15 +637,22 @@
         pltpu.SemaphoreType.DMA((moves, 4)),
         pltpu.SemaphoreType.DMA((2, n_narrow - 1)),
         pltpu.SemaphoreType.DMA((2, n_narrow - 1)),
+        pltpu.SemaphoreType.DMA((n_wide * n_narrow,)),
+        pltpu.SemaphoreType.DMA((n_wide * n_narrow,)),
+        pltpu.SemaphoreType.DMA,
     ]
     return pl.pallas_call(
         functools.partial(solve_kernel, n_wide, n_narrow),
-        out_shape=jax.ShapeDtypeStruct((X0, Y0, Z), jnp.float32),
+        out_shape=(
+            jax.ShapeDtypeStruct((X0, Y0, Z), jnp.float32),
+            jax.ShapeDtypeStruct(carried.shape, carried.dtype),
+        ),
         in_specs=[
             pl.BlockSpec(memory_space=pltpu.SMEM),
             pl.BlockSpec(memory_space=pltpu.VMEM),
+            pl.BlockSpec(memory_space=pl.ANY),
         ],
-        out_specs=pl.BlockSpec(memory_space=pltpu.VMEM),
+        out_specs=(pl.BlockSpec(memory_space=pltpu.VMEM), pl.BlockSpec(memory_space=pl.ANY)),
         scratch_shapes=scratch,
         compiler_params=pltpu.CompilerParams(
             collective_id=0, has_side_effects=True, vmem_limit_bytes=VMEM_LIMIT
@@ -574,7 +660,7 @@
         cost_estimate=pl.CostEstimate(
             flops=200_000_000, bytes_accessed=200_000_000, transcendentals=0
         ),
-    )(receive_index, arrived)
+    )(receive_index, arrived, carried)
 
 
 def shards(n_wide, n_narrow, target_slot, fields):
@@ -631,9 +717,7 @@
         tiled=True,
     )
     solved = swap(solved)
-    solved, carried = lax.optimization_barrier((solved, carried))
-    carried = swap(carried)
-    pressure = call_solve(n_wide, n_narrow, receive_index, solved)
+    pressure, carried = call_solve(n_wide, n_narrow, receive_index, solved, carried)
     migrated = pl.pallas_call(
         merge_kernel,
         out_shape=jax.ShapeDtypeStruct(fields.shape, fields.dtype),

time: 172 us -> 139 us (0.81); the launches traced: 170 us -> 138 us
  blocking collectives: 55 us -> 0 us
  waiting for transfers between devices: 0.01 us -> 46.7 us
  Pallas kernels: 103 us -> 78 us
  starting transfers between devices: 4.57 us -> 7.1 us
    all_to_all x1 -> x0, blocking collectives: 55 us -> none  [shards(): solved = swap(solved)]
    all_to_all x1, waiting for transfers between devices: 0.01 us -> 46.7 us  [shards(): solved = swap(solved)]
    pallas_call x1, Pallas kernels: 95 us -> 69.7 us  [call_solve(): pl.pallas_call(functools.partial(solve_kernel, n_wide, n_narrow), out_sha...]
    all_to_all x1, starting transfers between devices: 4.57 us -> 7.1 us  [shards(): solved = swap(solved)]
  transfers between devices with their start and end apart: 1 -> 1, of which waited for: 0 -> 1; matrix products, arithmetic and copies ran while one was open for 1% -> 1% of each run, Pallas kernels for 56% -> 0%
where the time goes in v3:
time: 139 us; the launch traced here: 138 us
  Pallas kernels  78 us (56%)
  waiting for transfers between devices  46.7 us (34%)
  starting transfers between devices  7.1 us (5%)
  other arithmetic  3.75 us (3%)
  local copies, waits for them, and re-layouts  2.24 us (2%)
    pallas_call x1, Pallas kernels, call_solve(): pl.pallas_call(functools.partial(solve_kernel, n_wide, n_narrow), out_sha...  69.7 us
    all_to_all x1, waiting for transfers between devices, shards(): solved = swap(solved)  46.7 us
    all_to_all x1, starting transfers between devices, shards(): solved = swap(solved)  7.1 us
    pallas_call x1, Pallas kernels, shards(): pl.pallas_call(merge_kernel, out_shape=jax.ShapeDtypeStruct(fields.shape,...  4.19 us
    pallas_call x1, Pallas kernels, shards(): pl.pallas_call(pack_kernel, out_shape=(jax.ShapeDtypeStruct((slots, SOLVE...  4.14 us
  transfers between devices with their start and end apart: 1, of which 1 were waited for; matrix products, arithmetic and copies ran while one was open for 1% of the time, Pallas kernels for 0%

profile of v3, /device:TPU:1, one launch (start us, length us, event | category | flops | bytes accessed | tf_op | source)
XLA Modules:
  0.0 138.5 jit_solution(4836591661769628691)
XLA Ops:
  0.6 0.8 and_select_fusion
  1.4 0.2 convert_reduce_fusion.1
  1.6 0.8 multiply_add_fusion
  2.4 0.6 select_reduce_fusion.1.index_ref
  3.0 4.1 %shard_map.41 = (bf16[64,4,4096]{2,1,0:T(4,128)(2,1)}, bf16[64,4,4096]{2,1,0:T(4,128)(2,1)}) custom-call(s32[64]{0:T(128)} %select_reduce_fusion.1.index_ref, bf16[32,8,4096]{2,1,0:T(8,128)(2,1)} %fields_ref.1), custom_call_target="tpu_custom_call" | custom-call | tf_op jit(solution)/shard_map/pallas_call | solution.py:702
  7.1 0.0 copy-start.2
  7.1 7.1 %all-to-all-start = ((bf16[64,4,4096]{2,1,0:T(4,128)(2,1)}), bf16[64,4,4096]{2,1,0:T(4,128)(2,1)S(1)}, u32[]{:S(2)}, u32[]{:S(2)}) async-start(bf16[64,4,4096]{2,1,0:T(4,128)(2,1)} %get-tuple-element.6), calls=%async_computation | async-start | bytes 4194304 | tf_op jit(solution)/shard_map/all_to_all | solution.py:719
  14.2 0.0 copy-done.2
  14.2 0.1 reshape.76
  14.3 0.6 convert_reduce_fusion
  14.9 0.1 broadcast_add_fusion
  15.0 0.1 add.45
  15.1 0.7 select_reduce_fusion.index_ref
  15.8 46.7 %all-to-all-done.arrived_ref.solved_ref = bf16[64,4,4096]{2,1,0:T(4,128)(2,1)S(1)} async-done(((bf16[64,4,4096]{2,1,0:T(4,128)(2,1)}), bf16[64,4,4096]{2,1,0:T(4,128)(2,1)S(1)}, u32[]{:S(2)}, u32[]{:S(2)}) %all-to-all-start) | async-done | bytes 2097184 | tf_op jit(solution)/shard_map/all_to_all | solution.py:719
  62.5 0.0 copy-start
  62.5 1.3 copy-done
  63.8 69.7 %shard_map.42 = (f32[16,64,128]{2,1,0:T(8,128)}, bf16[64,4,4096]{2,1,0:T(4,128)(2,1)}) custom-call(s32[32]{0:T(128)} %select_reduce_fusion.index_ref, bf16[64,4,4096]{2,1,0:T(4,128)(2,1)} %copy-done, bf16[64,4,4096]{2,1,0:T(4,128)(2,1)} %get-tuple-element.7.carried_ref), custom_call_target="tpu_custom_call" | custom-call | flops 200000000 | bytes 200000000 | tf_op jit(solution)/shard_map/pallas_call | solution.py:644
  133.5 0.0 copy-start.1
  133.5 4.2 %shard_map.43 = bf16[32,8,4096]{2,1,0:T(8,128)(2,1)} custom-call(s32[32]{0:T(128)} %select_reduce_fusion.index_ref, bf16[64,4,4096]{2,1,0:T(4,128)(2,1)} %copy-done, bf16[64,4,4096]{2,1,0:T(4,128)(2,1)} %get-tuple-element.8.carried_ref), custom_call_target="tpu_custom_call" | custom-call | tf_op jit(solution)/shard_map/pallas_call | solution.py:721
  137.7 0.0 copy-done.1
  137.7 0.8 copy.5
  (3 shorter events, 0.0 us)
Async XLA Ops:
  7.1 7.1 %copy-start.2 = (s32[1024]{0:T(1024)S(1)}, s32[1024]{0:T(1024)}, u32[]{:S(2)}) copy-start(s32[1024]{0:T(1024)} %param.2) | copy-start | bytes 12292
  7.1 55.4 %all-to-all-start = ((bf16[64,4,4096]{2,1,0:T(4,128)(2,1)}), bf16[64,4,4096]{2,1,0:T(4,128)(2,1)S(1)}, u32[]{:S(2)}, u32[]{:S(2)}) async-start(bf16[64,4,4096]{2,1,0:T(4,128)(2,1)} %get-tuple-element.6), calls=%async_computation | async-start | bytes 4194304 | tf_op jit(solution)/shard_map/all_to_all | solution.py:719
  62.5 1.3 copy-start
  133.5 4.2 %copy-start.1 = (f32[16,64,128]{2,1,0:T(8,128)S(1)}, f32[16,64,128]{2,1,0:T(8,128)}, u32[]{:S(2)}) copy-start(f32[16,64,128]{2,1,0:T(8,128)} %get-tuple-element.15) | copy-start | bytes 1572868

commit v4 on v3

--- a/solution.py
+++ b/solution.py
@@ -21,7 +21,7 @@
 Z = PATCH * BZP
 PAD = 8
 MESH = pl.DeviceIdType.MESH
-STRIDE = 13
+STRIDE = 15
 SHARES = (4,) + (2,) * 14
 VMEM_LIMIT = 60 * 1024 * 1024
 
@@ -54,9 +54,10 @@
     n_wide,
     n_narrow,
     index_ref,
-    arrived_ref,
+    solved_ref,
     carried_ref,
     out_ref,
+    arrived_ref,
     moved_ref,
     turn,
     tmp,
@@ -88,6 +89,8 @@
     carry_send_sem,
     carry_recv_sem,
     own_sem,
+    solved_send_sem,
+    solved_recv_sem,
 ):
     wide = lax.axis_index("wide")
     narrow = lax.axis_index("narrow")
@@ -150,8 +153,50 @@
             device_id_type=MESH,
         )
 
+    def solved_copy(k):
+        d = lax.rem(k * STRIDE, owners)
+        owner, device = owner_at(d)
+        return pltpu.make_async_remote_copy(
+            src_ref=solved_ref.at[block(owner)],
+            dst_ref=arrived_ref.at[block(me)],
+            send_sem=solved_send_sem.at[k],
+            recv_sem=solved_recv_sem.at[k],
+            device_id=device,
+            device_id_type=MESH,
+        )
+
+    def solved_landing(k):
+        d = lax.rem(k * STRIDE, owners)
+        _, device = owner_at(d)
+        came, _ = owner_at(owners - d)
+        return pltpu.make_async_remote_copy(
+            src_ref=solved_ref.at[block(me)],
+            dst_ref=arrived_ref.at[block(came)],
+            send_sem=solved_send_sem.at[k],
+            recv_sem=solved_recv_sem.at[k],
+            device_id=device,
+            device_id_type=MESH,
+        )
+
+    def solved_begin(k, carry):
+        solved_copy(k).start()
+        return carry
+
+    def solved_arrive(k, carry):
+        solved_landing(k).wait_recv()
+        return carry
+
+    def solved_end(k, carry):
+        solved_copy(k).wait_send()
+        return carry
+
+    lax.fori_loop(1, owners, solved_begin, 0)
+    own_solved = pltpu.make_async_copy(
+        solved_ref.at[block(me)], arrived_ref.at[block(me)], own_sem.at[1]
+    )
+    own_solved.start()
     own_copy = pltpu.make_async_copy(
-        carried_ref.at[block(me)], moved_ref.at[block(me)], own_sem
+        carried_ref.at[block(me)], moved_ref.at[block(me)], own_sem.at[0]
     )
     own_copy.start()
     shares = SHARES
@@ -170,6 +215,8 @@
 
         lax.fori_loop(bounds[turn_now], bounds[turn_now + 1], begin, 0)
 
+    own_solved.wait()
+    lax.fori_loop(1, owners, solved_arrive, 0)
     push()
 
     lane = lax.broadcasted_iota(jnp.int32, (8, Z), 1)
@@ -592,6 +639,7 @@
         return carry
 
     lax.fori_loop(1, owners, end, 0)
+    lax.fori_loop(1, owners, solved_end, 0)
     own_copy.wait()
     face_drain()
     source_drain()
@@ -603,7 +651,7 @@
     return pltpu.VMEM(shape, jnp.float32)
 
 
-def call_solve(n_wide, n_narrow, receive_index, arrived, carried):
+def call_solve(n_wide, n_narrow, receive_index, solved, carried):
     X3, Y3 = dims(LEVELS)
     levels = [dims(level) for level in range(LEVELS)]
     padded = f32(X0 + 2, Y0 + 2 * PAD, Z)
@@ -639,20 +687,27 @@
         pltpu.SemaphoreType.DMA((2, n_narrow - 1)),
         pltpu.SemaphoreType.DMA((n_wide * n_narrow,)),
         pltpu.SemaphoreType.DMA((n_wide * n_narrow,)),
-        pltpu.SemaphoreType.DMA,
+        pltpu.SemaphoreType.DMA((2,)),
+        pltpu.SemaphoreType.DMA((n_wide * n_narrow,)),
+        pltpu.SemaphoreType.DMA((n_wide * n_narrow,)),
     ]
     return pl.pallas_call(
         functools.partial(solve_kernel, n_wide, n_narrow),
         out_shape=(
             jax.ShapeDtypeStruct((X0, Y0, Z), jnp.float32),
+            jax.ShapeDtypeStruct(solved.shape, solved.dtype),
             jax.ShapeDtypeStruct(carried.shape, carried.dtype),
         ),
         in_specs=[
             pl.BlockSpec(memory_space=pltpu.SMEM),
+            pl.BlockSpec(memory_space=pl.ANY),
+            pl.BlockSpec(memory_space=pl.ANY),
+        ],
+        out_specs=(
+            pl.BlockSpec(memory_space=pltpu.VMEM),
             pl.BlockSpec(memory_space=pltpu.VMEM),
             pl.BlockSpec(memory_space=pl.ANY),
-        ],
-        out_specs=(pl.BlockSpec(memory_space=pltpu.VMEM), pl.BlockSpec(memory_space=pl.ANY)),
+        ),
         scratch_shapes=scratch,
         compiler_params=pltpu.CompilerParams(
             collective_id=0, has_side_effects=True, vmem_limit_bytes=VMEM_LIMIT
@@ -660,7 +715,7 @@
         cost_estimate=pl.CostEstimate(
             flops=200_000_000, bytes_accessed=200_000_000, transcendentals=0
         ),
-    )(receive_index, arrived, carried)
+    )(receive_index, solved, carried)
 
 
 def shards(n_wide, n_narrow, target_slot, fields):
@@ -709,15 +764,7 @@
         out_specs=(vmem, vmem),
         compiler_params=params,
     )(send_index, fields)
-    swap = functools.partial(
-        lax.all_to_all,
-        axis_name=("wide", "narrow"),
-        split_axis=0,
-        concat_axis=0,
-        tiled=True,
-    )
-    solved = swap(solved)
-    pressure, carried = call_solve(n_wide, n_narrow, receive_index, solved, carried)
+    pressure, solved, carried = call_solve(n_wide, n_narrow, receive_index, solved, carried)
     migrated = pl.pallas_call(
         merge_kernel,
         out_shape=jax.ShapeDtypeStruct(fields.shape, fields.dtype),

time: 139 us -> 136 us (0.978)
  Pallas kernels: 78 us -> 129 us
  waiting for transfers between devices: 46.7 us -> 0 us
  starting transfers between devices: 7.1 us -> 0 us
    pallas_call x1, Pallas kernels: 69.7 us -> 120 us  [call_solve(): pl.pallas_call(functools.partial(solve_kernel, n_wide, n_narrow), out_sha...]
    all_to_all x1 -> x0, waiting for transfers between devices: 46.7 us -> none  [shards(): solved = swap(solved)]
    all_to_all x1 -> x0, starting transfers between devices: 7.1 us -> none  [shards(): solved = swap(solved)]
  transfers between devices with their start and end apart: 1 -> 0, of which waited for: 1 -> 0; matrix products, arithmetic and copies ran while one was open for 1% -> 0% of each run, Pallas kernels for 0% -> 0%
where the time goes in v4:
time: 136 us; the launch traced here: 135 us
  Pallas kernels  129 us (95%)
  other arithmetic  4.45 us (3%)
  local copies, waits for them, and re-layouts  1.63 us (1%)
    pallas_call x1, Pallas kernels, call_solve(): pl.pallas_call(functools.partial(solve_kernel, n_wide, n_narrow), out_sha...  120 us
    pallas_call x1, Pallas kernels, shards(): pl.pallas_call(merge_kernel, out_shape=jax.ShapeDtypeStruct(fields.shape,...  4.19 us
    pallas_call x1, Pallas kernels, shards(): pl.pallas_call(pack_kernel, out_shape=(jax.ShapeDtypeStruct((slots, SOLVE...  4.14 us

profile of v4, /device:TPU:1, one launch (start us, length us, event | category | flops | bytes accessed | tf_op | source)
XLA Modules:
  0.0 135.3 jit_solution(10722138234183072607)
XLA Ops:
  0.6 0.8 and_select_fusion
  1.4 0.2 convert_reduce_fusion.1
  1.6 0.8 multiply_add_fusion
  2.4 0.6 select_reduce_fusion.1.index_ref
  3.0 0.8 reshape.76
  3.8 0.6 convert_reduce_fusion
  4.4 0.1 broadcast_add_fusion
  4.5 0.1 add.45
  4.5 1.4 %select_reduce_fusion.index_ref = s32[32]{0:T(128)} fusion(s32[1024]{0:T(1024)S(1)} %add.45, s32[1024]{0:T(1024)} %param.2, s32[32]{0:T(128)S(1)} %iota_add_fusion), kind=kLoop, calls=%fused_computation.1 | loop fusion | flops 98272 | bytes 8448 | tf_op jit(solution)/shard_map/reduce_sum | solution.py:746
  5.9 4.1 %shard_map.41 = (bf16[64,4,4096]{2,1,0:T(4,128)(2,1)}, bf16[64,4,4096]{2,1,0:T(4,128)(2,1)}) custom-call(s32[64]{0:T(128)} %select_reduce_fusion.1.index_ref, bf16[32,8,4096]{2,1,0:T(8,128)(2,1)} %fields_ref.1), custom_call_target="tpu_custom_call" | custom-call | tf_op jit(solution)/shard_map/pallas_call | solution.py:757
  10.1 120.2 %shard_map.42 = (f32[16,64,128]{2,1,0:T(8,128)}, bf16[64,4,4096]{2,1,0:T(4,128)(2,1)}, bf16[64,4,4096]{2,1,0:T(4,128)(2,1)}) custom-call(s32[32]{0:T(128)} %select_reduce_fusion.index_ref, bf16[64,4,4096]{2,1,0:T(4,128)(2,1)} %get-tuple-element.7.solved_ref, bf16[64,4,4096]{2,1,0:T(4,128)(2,1)} %get-tuple-element.8.carried_ref), custom_call_target="tpu_custom_call" | custom-call | flops 200000000 | bytes 200000000 | tf_op jit(solution)/shard_map/pallas_call | solution.py:694
  130.3 0.0 copy-start
  130.3 4.2 %shard_map.43 = bf16[32,8,4096]{2,1,0:T(8,128)(2,1)} custom-call(s32[32]{0:T(128)} %select_reduce_fusion.index_ref, bf16[64,4,4096]{2,1,0:T(4,128)(2,1)} %get-tuple-element.9.solved_ref, bf16[64,4,4096]{2,1,0:T(4,128)(2,1)} %get-tuple-element.10.carried_ref), custom_call_target="tpu_custom_call" | custom-call | tf_op jit(solution)/shard_map/pallas_call | solution.py:768
  134.5 0.0 copy-done
  134.5 0.8 copy.5
  (3 shorter events, 0.0 us)
Async XLA Ops:
  130.3 4.2 %copy-start = (f32[16,64,128]{2,1,0:T(8,128)S(1)}, f32[16,64,128]{2,1,0:T(8,128)}, u32[]{:S(2)}) copy-start(f32[16,64,128]{2,1,0:T(8,128)} %get-tuple-element.17) | copy-start | bytes 1572868

commit v5 on v4

--- a/solution.py
+++ b/solution.py
@@ -22,7 +22,7 @@
 PAD = 8
 MESH = pl.DeviceIdType.MESH
 STRIDE = 15
-SHARES = (4,) + (2,) * 14
+SHARES = (4, 3, 3) + (2,) * 10 + (1, 0)
 VMEM_LIMIT = 60 * 1024 * 1024
 
 
@@ -37,7 +37,7 @@
         carried_ref[slot] = patch[SOLVED:]
         return carry
 
-    lax.fori_loop(0, solved_ref.shape[0], one, 0, unroll=4)
+    lax.fori_loop(0, solved_ref.shape[0], one, 0, unroll=8)
 
 
 def merge_kernel(index_ref, solved_ref, carried_ref, out_ref):
@@ -47,7 +47,7 @@
         out_ref[patch, SOLVED:] = carried_ref[row]
         return carry
 
-    lax.fori_loop(0, out_ref.shape[0], one, 0, unroll=4)
+    lax.fori_loop(0, out_ref.shape[0], one, 0, unroll=8)
 
 
 def solve_kernel(
@@ -254,7 +254,7 @@
                     ref[i + 1, pl.ds(PAD + y, 8), :] = values
         return carry
 
-    lax.fori_loop(0, BYP * X0, to_grid, 0, unroll=4)
+    lax.fori_loop(0, BYP * X0, to_grid, 0, unroll=8)
 
     def exchange(padded, X, Y, sent, got, slot, sides):
         mid = pl.ds(PAD, Y)
@@ -607,7 +607,7 @@
         new += coef[5] * pltpu.roll(cur, Z - step, 2)
         return new
 
-    coef[7] = lax.fori_loop(0, BOTTOM - 1, bottom, coef[6], unroll=3)
+    coef[7] = lax.fori_loop(0, BOTTOM - 1, bottom, coef[6], unroll=15)
     for x in range(X):
         answer[LEVELS][x] = coef[7, narrow * X + x]
 

time: 136 us -> 134 us (0.985)
  Pallas kernels: 129 us -> 126 us
    pallas_call x1, Pallas kernels: 120 us -> 118 us  [call_solve(): pl.pallas_call(functools.partial(solve_kernel, n_wide, n_narrow), out_sha...]
where the time goes in v5:
time: 134 us; the launch traced here: 133 us
  Pallas kernels  126 us (94%)
  other arithmetic  4.45 us (3%)
  local copies, waits for them, and re-layouts  1.63 us (1%)
    pallas_call x1, Pallas kernels, call_solve(): pl.pallas_call(functools.partial(solve_kernel, n_wide, n_narrow), out_sha...  118 us
    pallas_call x1, Pallas kernels, shards(): pl.pallas_call(merge_kernel, out_shape=jax.ShapeDtypeStruct(fields.shape,...  4.17 us
    pallas_call x1, Pallas kernels, shards(): pl.pallas_call(pack_kernel, out_shape=(jax.ShapeDtypeStruct((slots, SOLVE...  4.09 us

profile of v5, /device:TPU:1, one launch (start us, length us, event | category | flops | bytes accessed | tf_op | source)
XLA Modules:
  0.0 132.5 jit_solution(15719626455840530079)
XLA Ops:
  0.6 0.8 and_select_fusion
  1.4 0.2 convert_reduce_fusion.1
  1.6 0.8 multiply_add_fusion
  2.4 0.6 select_reduce_fusion.1.index_ref
  3.0 0.8 reshape.76
  3.8 0.6 convert_reduce_fusion
  4.4 0.1 broadcast_add_fusion
  4.5 0.1 add.45
  4.5 1.4 %select_reduce_fusion.index_ref = s32[32]{0:T(128)} fusion(s32[1024]{0:T(1024)S(1)} %add.45, s32[1024]{0:T(1024)} %param.2, s32[32]{0:T(128)S(1)} %iota_add_fusion), kind=kLoop, calls=%fused_computation.1 | loop fusion | flops 98272 | bytes 8448 | tf_op jit(solution)/shard_map/reduce_sum | solution.py:746
  5.9 4.1 %shard_map.41 = (bf16[64,4,4096]{2,1,0:T(4,128)(2,1)}, bf16[64,4,4096]{2,1,0:T(4,128)(2,1)}) custom-call(s32[64]{0:T(128)} %select_reduce_fusion.1.index_ref, bf16[32,8,4096]{2,1,0:T(8,128)(2,1)} %fields_ref.1), custom_call_target="tpu_custom_call" | custom-call | tf_op jit(solution)/shard_map/pallas_call | solution.py:757
  10.0 117.5 %shard_map.42 = (f32[16,64,128]{2,1,0:T(8,128)}, bf16[64,4,4096]{2,1,0:T(4,128)(2,1)}, bf16[64,4,4096]{2,1,0:T(4,128)(2,1)}) custom-call(s32[32]{0:T(128)} %select_reduce_fusion.index_ref, bf16[64,4,4096]{2,1,0:T(4,128)(2,1)} %get-tuple-element.7.solved_ref, bf16[64,4,4096]{2,1,0:T(4,128)(2,1)} %get-tuple-element.8.carried_ref), custom_call_target="tpu_custom_call" | custom-call | flops 200000000 | bytes 200000000 | tf_op jit(solution)/shard_map/pallas_call | solution.py:694
  127.6 0.0 copy-start
  127.6 4.2 %shard_map.43 = bf16[32,8,4096]{2,1,0:T(8,128)(2,1)} custom-call(s32[32]{0:T(128)} %select_reduce_fusion.index_ref, bf16[64,4,4096]{2,1,0:T(4,128)(2,1)} %get-tuple-element.9.solved_ref, bf16[64,4,4096]{2,1,0:T(4,128)(2,1)} %get-tuple-element.10.carried_ref), custom_call_target="tpu_custom_call" | custom-call | tf_op jit(solution)/shard_map/pallas_call | solution.py:768
  131.7 0.0 copy-done
  131.7 0.8 copy.5
  (3 shorter events, 0.0 us)
Async XLA Ops:
  127.6 4.2 %copy-start = (f32[16,64,128]{2,1,0:T(8,128)S(1)}, f32[16,64,128]{2,1,0:T(8,128)}, u32[]{:S(2)}) copy-start(f32[16,64,128]{2,1,0:T(8,128)} %get-tuple-element.17) | copy-start | bytes 1572868
